TPU v7x, 256 devices: a whole 4x4x8 slice. The times are simulated.
256 devices in a mesh: dom: 64 (over x, z, core), feat: 4 (over y).
Axes of the slice: x: 4, y: 4, z: 8, core: 2. Of those that a mesh axis runs over, the one named last changes fastest.
Arguments:
- features: bfloat16 [65536, 1024], P('dom', 'feat'), may hold values from -6 to 6
- adjacency: bfloat16 [512, 16, 128, 128], P('dom'), may hold values from -0.125 to 0.125
- tile_src: int32 [512, 16], replicated, may hold values from 0 to 511, as said below
- mig_slot: int32 [64, 2], replicated, may hold values from 0 to 7, as said below
- weight_one: bfloat16 [1024, 1024], replicated, may hold values from -0.1875 to 0.1875
- weight_two: bfloat16 [1024, 1024], replicated, may hold values from -0.1875 to 0.1875
Outputs:
- mixed: bfloat16 [65536, 1024], P('dom', 'feat')
Inputs may be any that keep to these rules, and one draw needn't show every extreme that they name: `tile_src`: the tiles of the row blocks that one partition holds name at most 2 distinct blocks held by any one other partition, both in the starting placement and in the placement after the move; in the starting placement they name exactly 2 blocks of every other partition, one of which leaves that partition in the move. `mig_slot`: each row holds 2 distinct slots.
All inputs are finite; a program needn't handle non-finite values.
Results may differ from a plain program's by a relative error of at most 0.0064.
Values may be sent and summed in bfloat16 or wider, within the bound.
A program may use at most 128 MiB of HBM per device.

v0:
```python
import jax
import jax.numpy as jnp
from jax import lax
from jax.sharding import PartitionSpec as P

B = 128
R = 8
TPB = 16
CAP = 2


def joined_along(pieces, dim):
    pieces = jnp.moveaxis(pieces, 0, dim)
    dims = pieces.shape
    return pieces.reshape(*dims[:dim], dims[dim] * dims[dim + 1], *dims[dim + 2 :])


def copy_for_each(value, axis):
    count = lax.axis_size(axis)
    return lax.all_to_all(
        jnp.broadcast_to(value[None], (count, *value.shape)), axis, 0, 0, tiled=True
    )


def collect(value, axis, dim):
    return joined_along(copy_for_each(value, axis), dim)


def from_behind(value, axis, by):
    count = lax.axis_size(axis)
    return lax.ppermute(value, axis, [(i, (i + by) % count) for i in range(count)])


def place_blocks(sources, mig_slot, after_move):
    domains = mig_slot.shape[0]
    holders = sources // R
    slot_ids = sources % R
    if not after_move:
        return (holders, slot_ids)
    marked = jnp.take(mig_slot, holders, axis=0)
    matches = marked == slot_ids[..., None]
    is_moved = jnp.any(matches, axis=-1)
    successor = (holders + 1) % domains
    landing = jnp.take(mig_slot, successor, axis=0)
    new_slot = jnp.sum(jnp.where(matches, landing, 0), axis=-1)
    return (jnp.where(is_moved, successor, holders), jnp.where(is_moved, new_slot, slot_ids))


def request_tables(holders, slot_ids):
    domains = holders.shape[0]
    my_index = lax.axis_index("dom")
    domain_ids = jnp.arange(domains, dtype=jnp.int32)
    not_self = (holders != domain_ids[:, None]).astype(jnp.float32)
    peer_hot = (holders[:, :, None] == domain_ids[None, None, :]).astype(jnp.float32) * not_self[
        :, :, None
    ]
    slot_hot = (slot_ids[:, :, None] == jnp.arange(R, dtype=jnp.int32)[None, None, :]).astype(
        jnp.float32
    )
    needed = (jnp.einsum("ptq,pts->pqs", peer_hot, slot_hot) > 0.5).astype(jnp.int32)
    rank_of = jnp.cumsum(needed, axis=2) - 1
    picked = (needed[..., None] == 1) & (rank_of[..., None] == jnp.arange(CAP, dtype=jnp.int32))
    requests = jnp.sum(
        picked.astype(jnp.int32) * jnp.arange(R, dtype=jnp.int32)[None, None, :, None], axis=2
    )
    send_slots = requests[:, my_index, :]
    my_holders = holders[my_index]
    my_slot_ids = slot_ids[my_index]
    my_ranks = rank_of[my_index]
    position = my_ranks[my_holders, my_slot_ids]
    tile_index = jnp.where(my_holders == my_index, my_slot_ids, R + my_holders * CAP + position)
    return (send_slots, tile_index)


def aggregate(local_blocks, adjacency, send_slots, tile_index):
    col_width = local_blocks.shape[2]
    outgoing = local_blocks[send_slots]
    arrived = lax.all_to_all(outgoing, "dom", split_axis=0, concat_axis=0, tiled=True)
    block_pool = jnp.concatenate([local_blocks, arrived.reshape(-1, B, col_width)], axis=0)
    sources = block_pool[tile_index].reshape(R, TPB, B, col_width)
    return jnp.einsum("rtij,rtjf->rif", adjacency, sources, preferred_element_type=jnp.float32)


def transform(summed, weight):
    col_width = summed.shape[2]
    agg_rows = summed.astype(jnp.bfloat16).reshape(R * B, col_width)
    feat_index = lax.axis_index("feat")
    col_slice = lax.dynamic_slice_in_dim(weight, feat_index * col_width, col_width, 1)
    return jnp.dot(collect(agg_rows, "feat", 1), col_slice, preferred_element_type=jnp.float32)


def on_device(features, adjacency, tile_src, mig_slot, weight_one, weight_two):
    domains = lax.axis_size("dom")
    my_index = lax.axis_index("dom")
    col_width = features.shape[1]
    local_blocks = features.reshape(R, B, col_width)
    old_sources = tile_src.reshape(domains, R * TPB)
    holders, slot_ids = place_blocks(old_sources, mig_slot, False)
    send_slots, tile_index = request_tables(holders, slot_ids)
    layer_one = aggregate(local_blocks, adjacency, send_slots, tile_index)
    hidden = (
        jax.nn.relu(transform(layer_one, weight_one)).astype(jnp.bfloat16).reshape(R, B, col_width)
    )
    my_slots = mig_slot[my_index]
    leaving = hidden[my_slots]
    leaving_tiles = adjacency[my_slots]
    per_core = TPB // lax.axis_size("feat")
    tile_piece = lax.dynamic_slice_in_dim(
        leaving_tiles, lax.axis_index("feat") * per_core, per_core, 1
    )
    moved_rows, moved_piece = from_behind((leaving, tile_piece), "dom", 1)
    moved_tiles = collect(moved_piece, "feat", 1)
    new_hidden = hidden.at[my_slots].set(moved_rows)
    new_tiles = adjacency.at[my_slots].set(moved_tiles)
    domain_ids = jnp.arange(domains, dtype=jnp.int32)
    block_ids = domain_ids[:, None] * R + jnp.arange(R, dtype=jnp.int32)[None, :]
    previous = ((domain_ids - 1) % domains * R)[:, None] + jnp.roll(mig_slot, 1, axis=0)
    new_ids = block_ids.at[domain_ids[:, None], mig_slot].set(previous)
    new_sources = tile_src[new_ids.reshape(-1)].reshape(domains, R * TPB)
    holders_two, slot_ids_two = place_blocks(new_sources, mig_slot, True)
    send_two, index_two = request_tables(holders_two, slot_ids_two)
    layer_two = aggregate(new_hidden, new_tiles, send_two, index_two)
    return transform(layer_two, weight_two).astype(jnp.bfloat16)


def solution(mesh):
    in_specs = (P("dom", "feat"), P("dom", None, None, None), P(), P(), P(), P())
    out_specs = P("dom", "feat")
    return jax.shard_map(
        on_device, mesh=mesh, in_specs=in_specs, out_specs=out_specs, check_vma=False
    )
```

profile of v0, /device:TPU:8, one launch (start us, length us, event | category | flops | bytes accessed | tf_op | source)
XLA Modules:
  0.0 615.5 jit_solution(13868825755558819631)
XLA Ops:
  0.0 4.9 copy.84
  6.3 6.4 %scatter_fusion.2 = s32[64,8]{0,1:T(8,128)S(1)} fusion(s32[64,8]{0,1:T(8,128)S(1)} %iota_add_fusion, s32[128]{0:T(128)S(1)} %reshape.670, s32[128]{0:T(128)S(1)} %reshape.672), kind=kCustom, calls=%fused_computation.13 | custom fusion | bytes 2560 | tf_op jit(solution)/shard_map/scatter | solution.py:118
  14.7 28.0 %gather_fusion.9 = s32[8192,2]{1,0:T(8,128)} fusion(s32[64,2]{1,0:T(8,128)S(1)} %copy.73, s32[8192]{0:T(1024)S(1)} %get-tuple-element.14), kind=kCustom, calls=%fused_computation.clone | custom fusion | bytes 163840 | tf_op jit(solution)/shard_map/jit(_take)/gather | solution.py:40
  42.6 27.9 %gather_fusion.10 = s32[8192,2]{1,0:T(8,128)} fusion(s32[64,2]{1,0:T(8,128)S(1)} %copy.73, s32[8192]{0:T(1024)S(1)} %get-tuple-element.15), kind=kCustom, calls=%fused_computation.1.clone | custom fusion | bytes 163840 | tf_op jit(solution)/shard_map/jit(_take)/gather | solution.py:44
  70.5 7.5 %fusion = (s32[64,128]{1,0:T(8,128)S(1)}, pred[64,128,2]{2,1,0:T(8,128)(4,1)S(1)}) fusion(s32[64,128,2]{2,1,0:T(8,128)} %bitcast.120, pred[64,128]{1,0:T(8,128)(4,1)S(1)} %get-tuple-element.13, s32[64,128]{1,0:T(8,128)S(1)} %add_select_fusion.1, s32[64,128,2]{2,1,0:T(8,128)} %bitcast.119, pred[64,128]{1,0:T(8,128)(4,1)S(1)} %get-tuple-element.12), kind=kLoop, calls=%fused_computation.17 | loop fusion | flops 73728 | bytes 229376 | tf_op jit(solution)/shard_map/reduce_sum | solution.py:45
  82.5 6.5 %gather_fusion.1 = bf16[128,128,256]{2,1,0:T(8,128)(2,1)} fusion(bf16[8,128,256]{2,1,0:T(8,128)(2,1)S(1)} %bitcast.113, s32[1024]{0:T(1024)S(1)} %pad_clamp_fusion.4), kind=kCustom, calls=%fused_computation.3 | custom fusion | bytes 16777728 | tf_op jit(solution)/shard_map/gather | solution.py:77
  89.1 12.4 %all-to-all-start.1 = ((bf16[64,2,128,256]{3,2,1,0:T(8,128)(2,1)}), bf16[64,2,128,256]{3,2,1,0:T(8,128)(2,1)}, u32[]{:S(2)}, u32[]{:S(2)}) async-start(bf16[64,2,128,256]{3,2,1,0:T(8,128)(2,1)} %bitcast.118), calls=%async_computation.1 | async-start | bytes 16777216 | tf_op jit(solution)/shard_map/all_to_all | solution.py:78
  103.9 182.2 %all-to-all-done.1 = bf16[64,2,128,256]{3,2,1,0:T(8,128)(2,1)} async-done(((bf16[64,2,128,256]{3,2,1,0:T(8,128)(2,1)}), bf16[64,2,128,256]{3,2,1,0:T(8,128)(2,1)}, u32[]{:S(2)}, u32[]{:S(2)}) %all-to-all-start.1) | async-done | bytes 8388640 | tf_op jit(solution)/shard_map/all_to_all | solution.py:78
  286.1 7.5 %pad_maximum_fusion = bf16[136,128,256]{2,1,0:T(8,128)(2,1)} fusion(bf16[128,128,256]{2,1,0:T(8,128)(2,1)} %bitcast.6, bf16[8,128,256]{2,1,0:T(8,128)(2,1)S(1)} %bitcast.114), kind=kLoop, calls=%fused_computation.14 | loop fusion | flops 4456448 | bytes 17825792 | tf_op jit(solution)/shard_map/concatenate | solution.py:79
  293.7 10.2 %gather_fusion.3 = bf16[128,128,256]{2,1,0:T(8,128)(2,1)} fusion(bf16[136,128,256]{2,1,0:T(8,128)(2,1)} %pad_maximum_fusion, s32[1024]{0:T(1024)S(1)} %pad_clamp_fusion.3), kind=kCustom, calls=%fused_computation.5 | custom fusion | bytes 16777728 | tf_op jit(solution)/shard_map/gather | solution.py:80
  303.8 6.0 fusion.7
  311.7 4.9 all-to-all-start.2
  316.6 3.9 gather_fusion
  322.1 8.6 %collective-permute-done = bf16[2,4,128,128]{3,2,1,0:T(8,128)(2,1)S(1)} collective-permute-done((bf16[2,4,128,128]{3,2,1,0:T(8,128)(2,1)S(1)}, bf16[2,4,128,128]{3,2,1,0:T(8,128)(2,1)S(1)}, u32[]{:S(2)}, u32[]{:S(2)}) %collective-permute-start) | collective-permute-done | bytes 262176 | tf_op jit(solution)/shard_map/ppermute | solution.py:31
  330.7 12.2 %all-to-all-done.2 = bf16[4,1024,256]{1,2,0:T(8,128)(2,1)} async-done(((bf16[4,1024,256]{1,2,0:T(8,128)(2,1)}), bf16[4,1024,256]{1,2,0:T(8,128)(2,1)}, u32[]{:S(2)}, u32[]{:S(2)}) %all-to-all-start.2) | async-done | bytes 2097184 | tf_op jit(solution)/shard_map/all_to_all | solution.py:20
  344.2 5.6 all-to-all-start
  353.0 7.4 %collective-permute-done.1 = bf16[2,128,256]{2,1,0:T(8,128)(2,1)S(1)} collective-permute-done((bf16[2,128,256]{2,1,0:T(8,128)(2,1)S(1)}, bf16[2,128,256]{2,1,0:T(8,128)(2,1)S(1)}, u32[]{:S(2)}, u32[]{:S(2)}) %collective-permute-start.1) | collective-permute-done | bytes 131104 | tf_op jit(solution)/shard_map/ppermute | solution.py:31
  361.1 6.5 %gather_fusion.6 = bf16[128,128,256]{2,1,0:T(8,128)(2,1)} fusion(bf16[8,128,256]{2,1,0:T(8,128)(2,1)S(1)} %scatter_fusion.1, s32[1024]{0:T(1024)S(1)} %pad_clamp_fusion.1), kind=kCustom, calls=%fused_computation.8 | custom fusion | bytes 16777728 | tf_op jit(solution)/shard_map/gather | solution.py:77
  367.6 6.0 all-to-all-start.3
  380.8 177.5 %all-to-all-done.3 = bf16[64,2,128,256]{3,2,1,0:T(8,128)(2,1)} async-done(((bf16[64,2,128,256]{3,2,1,0:T(8,128)(2,1)}), bf16[64,2,128,256]{3,2,1,0:T(8,128)(2,1)}, u32[]{:S(2)}, u32[]{:S(2)}) %all-to-all-start.3) | async-done | bytes 8388640 | tf_op jit(solution)/shard_map/all_to_all | solution.py:78
  558.2 7.5 %pad_maximum_fusion.1 = bf16[136,128,256]{2,1,0:T(8,128)(2,1)} fusion(bf16[128,128,256]{2,1,0:T(8,128)(2,1)} %bitcast.29, bf16[8,128,256]{2,1,0:T(8,128)(2,1)S(1)} %scatter_fusion.1), kind=kLoop, calls=%fused_computation.15 | loop fusion | flops 4456448 | bytes 17825792 | tf_op jit(solution)/shard_map/concatenate | solution.py:79
  565.8 10.2 %gather_fusion.8 = bf16[128,128,256]{2,1,0:T(8,128)(2,1)} fusion(bf16[136,128,256]{2,1,0:T(8,128)(2,1)} %pad_maximum_fusion.1, s32[1024]{0:T(1024)S(1)} %pad_clamp_fusion), kind=kCustom, calls=%fused_computation.10 | custom fusion | bytes 16777728 | tf_op jit(solution)/shard_map/gather | solution.py:80
  575.9 6.0 fusion.6
  582.5 30.4 %all_to_all.25 = bf16[4,1024,256]{1,2,0:T(8,128)(2,1)S(1)} all-to-all(bf16[4,1024,256]{1,2,0:T(8,128)(2,1)S(1)} %broadcast_in_dim.30), channel_id=1, replica_groups=mesh['dom'=64,'feat'=4] {'feat'}, dimensions={0} | all-to-all | bytes 4194304 | tf_op jit(solution)/shard_map/all_to_all | solution.py:20
  (89 shorter events, 28.9 us)
Async XLA Ops:
  0.0 349.8 %copy-start = (bf16[1024,1024]{1,0:T(8,128)(2,1)S(1)}, bf16[1024,1024]{1,0:T(8,128)(2,1)}, u32[]{:S(2)}) copy-start(bf16[1024,1024]{1,0:T(8,128)(2,1)} %param.12) | copy-start | bytes 6291460
  0.0 4.9 copy-start.7
  6.3 6.7 %copy-start.6 = (s32[512,16]{0,1:T(8,128)S(1)}, s32[512,16]{0,1:T(8,128)}, u32[]{:S(2)}) copy-start(s32[512,16]{0,1:T(8,128)} %param.10) | copy-start | bytes 98308
  14.6 65.6 %copy-start.3 = (s32[64,128]{1,0:T(8,128)}, s32[64,128]{1,0:T(8,128)S(1)}, u32[]{:S(2)}) copy-start(s32[64,128]{1,0:T(8,128)S(1)} %get-tuple-element.11) | copy-start | bytes 98308
  14.6 65.6 %copy-start.4 = (s32[64,128]{1,0:T(8,128)}, s32[64,128]{1,0:T(8,128)S(1)}, u32[]{:S(2)}) copy-start(s32[64,128]{1,0:T(8,128)S(1)} %add_select_fusion.3) | copy-start | bytes 98308
  79.2 1.7 copy-start.5
  79.3 1.6 copy-start.2
  79.3 3.3 copy-start.1
  89.1 197.1 %all-to-all-start.1 = ((bf16[64,2,128,256]{3,2,1,0:T(8,128)(2,1)}), bf16[64,2,128,256]{3,2,1,0:T(8,128)(2,1)}, u32[]{:S(2)}, u32[]{:S(2)}) async-start(bf16[64,2,128,256]{3,2,1,0:T(8,128)(2,1)} %bitcast.118), calls=%async_computation.1 | async-start | bytes 16777216 | tf_op jit(solution)/shard_map/all_to_all | solution.py:78
  309.9 6.8 %copy-start.8 = (s32[2]{0:T(128)S(1)}, s32[2]{0:T(128)}, u32[]{:S(2)}) copy-start(s32[2]{0:T(128)} %get-tuple-element.17) | copy-start | bytes 28
  311.7 31.2 %all-to-all-start.2 = ((bf16[4,1024,256]{1,2,0:T(8,128)(2,1)}), bf16[4,1024,256]{1,2,0:T(8,128)(2,1)}, u32[]{:S(2)}, u32[]{:S(2)}) async-start(bf16[4,1024,256]{1,2,0:T(8,128)(2,1)} %broadcast_in_dim.25), calls=%async_computation.2 | async-start | bytes 4194304 | tf_op jit(solution)/shard_map/all_to_all | solution.py:20
  321.5 9.2 %collective-permute-start = (bf16[2,4,128,128]{3,2,1,0:T(8,128)(2,1)S(1)}, bf16[2,4,128,128]{3,2,1,0:T(8,128)(2,1)S(1)}, u32[]{:S(2)}, u32[]{:S(2)}) collective-permute-start(bf16[2,4,128,128]{3,2,1,0:T(8,128)(2,1)S(1)} %constant_dynamic-slice_fusion.6), channel_id=1, source_target_pairs={{0,4},{4,8},{8,12},{12,16},{16,20},{20,24},{24,28},{28,32},{32,36}... | collective-permute-start | bytes 786440 | tf_op jit(solution)/shard_map/ppermute | solution.py:31
  344.2 23.4 %all-to-all-start = ((bf16[4,2,4,128,128]{4,3,2,1,0:T(8,128)(2,1)}), bf16[4,2,4,128,128]{4,3,2,1,0:T(8,128)(2,1)}, u32[]{:S(2)}, u32[]{:S(2)}) async-start(bf16[4,2,4,128,128]{4,3,2,1,0:T(8,128)(2,1)} %broadcast_in_dim.23), calls=%async_computation | async-start | bytes 2097152 | tf_op jit(solution)/shard_map/all_to_all | solution.py:20
  352.7 7.8 %collective-permute-start.1 = (bf16[2,128,256]{2,1,0:T(8,128)(2,1)S(1)}, bf16[2,128,256]{2,1,0:T(8,128)(2,1)S(1)}, u32[]{:S(2)}, u32[]{:S(2)}) collective-permute-start(bf16[2,128,256]{2,1,0:T(8,128)(2,1)S(1)} %gather_fusion.4), channel_id=1, source_target_pairs={{0,4},{4,8},{8,12},{12,16},{16,20},{20,24},{24,28},{28,32},{32,36}... | collective-permute-start | bytes 393224 | tf_op jit(solution)/shard_map/ppermute | solution.py:31
  367.6 190.6 %all-to-all-start.3 = ((bf16[64,2,128,256]{3,2,1,0:T(8,128)(2,1)}), bf16[64,2,128,256]{3,2,1,0:T(8,128)(2,1)}, u32[]{:S(2)}, u32[]{:S(2)}) async-start(bf16[64,2,128,256]{3,2,1,0:T(8,128)(2,1)} %bitcast.117), calls=%async_computation.3 | async-start | bytes 16777216 | tf_op jit(solution)/shard_map/all_to_all | solution.py:78
where the time goes:
time: 618 us; the launch traced here: 616 us
  waiting for transfers between devices  388 us (63%)
  local copies, waits for them, and re-layouts  121 us (20%)
  blocking collectives  30.4 us (5%)
  starting transfers between devices  29.5 us (5%)
  other arithmetic  27.4 us (4%)
  matrix products  18.3 us (3%)
    all_to_all x2, waiting for transfers between devices, aggregate(): lax.all_to_all(outgoing, 'dom', split_axis=0, concat_axis=0, tiled=True)  360 us
    all_to_all x1, blocking collectives, copy_for_each(): lax.all_to_all(jnp.broadcast_to(value[None], (count, *value.shape)), axis...  30.4 us
    gather x1, local copies, waits for them, and re-layouts, place_blocks(): marked = jnp.take(mig_slot, holders, axis=0)  28 us
    gather x1, local copies, waits for them, and re-layouts, place_blocks(): landing = jnp.take(mig_slot, successor, axis=0)  27.9 us
    gather x2, local copies, waits for them, and re-layouts, aggregate(): sources = block_pool[tile_index].reshape(R, TPB, B, col_width)  20.3 us
    all_to_all x2, starting transfers between devices, aggregate(): lax.all_to_all(outgoing, 'dom', split_axis=0, concat_axis=0, tiled=True)  18.3 us
    ppermute x2, waiting for transfers between devices, from_behind(): lax.ppermute(value, axis, [(i, (i + by) % count) for i in range(count)])  16 us
    concatenate x2, other arithmetic, aggregate(): jnp.concatenate([local_blocks, arrived.reshape(-1, B, col_width)], axis=0)  15.1 us
  transfers between devices with their start and end apart: 6, of which 5 were waited for; matrix products, arithmetic and copies ran while one was open for 4% of the time, Pallas kernels for 0%

commit v1 on v0

v1 whole, which is shorter than its diff:
```python
import functools

import jax
import jax.numpy as jnp
from jax import lax
from jax.experimental import pallas as pl
from jax.experimental.pallas import tpu as pltpu
from jax.sharding import PartitionSpec as P

B = 128
R = 8
TPB = 16
NX, NZ, NC, NY = 4, 8, 2, 4
COLS = 256
ROWS = R * B
TILES = R * TPB
CAP = 34
LIST = 48
MESH = pl.DeviceIdType.MESH
BF, F32 = jnp.bfloat16, jnp.float32
VMEM_LIMIT = 60 * 1024 * 1024


class Place:
    def __init__(self):
        d = lax.axis_index("dom")
        self.dom = d
        self.y = lax.axis_index("feat")
        self.x = d // (NZ * NC)
        self.z = lax.rem(d // NC, NZ)
        self.c = lax.rem(d, NC)

    def at(self, dx=0, dz=0, sibling=False, dy=0):
        x = lax.rem(self.x + (dx + NX), NX)
        z = lax.rem(self.z + (dz + NZ), NZ)
        c = 1 - self.c if sibling else self.c
        y = lax.rem(self.y + (dy + NY), NY)
        return ((x * NZ + z) * NC + c, y)

    def ring(self, by):
        return (lax.rem(self.dom + (by + NX * NZ * NC), NX * NZ * NC), self.y)


def meet(partners, come_from):
    barrier = pltpu.get_barrier_semaphore()
    for p in partners:
        pl.semaphore_signal(barrier, inc=1, device_id=p, device_id_type=MESH)
    pl.semaphore_wait(barrier, come_from)


def remote(src, dst, send, recv, device):
    return pltpu.make_async_remote_copy(
        src_ref=src, dst_ref=dst, send_sem=send, recv_sem=recv, device_id=device, device_id_type=MESH
    )


def pack_kernel(src_ref, adj_ref, send_ref, own_ref, list_ref, start_ref, adj, sem):
    x = lax.axis_index("dom") // (NZ * NC)
    y = lax.axis_index("feat")
    load = pltpu.make_async_copy(adj_ref, adj, sem)
    load.start()
    send_ref[...] = jnp.zeros_like(send_ref)
    own_ref[...] = jnp.zeros_like(own_ref)

    def row(r, counts):
        for p in range(NX):
            start_ref[p * 16 + r] = counts[p]

        def tile(j, counts):
            t = r * TPB + j
            new = []
            for p in range(NX):
                s = src_ref[p * TILES + t]
                list_ref[p * LIST + counts[p]] = t * TILES + lax.rem(s, 128)
                new.append(counts[p] + jnp.where(s // 128 == x, 1, 0))
            return tuple(new)

        return lax.fori_loop(0, TPB, tile, counts, unroll=4)

    zero = jnp.int32(0)
    counts = lax.fori_loop(0, R, row, (zero,) * NX)
    for p in range(NX):
        start_ref[p * 16 + R] = counts[p]
    load.wait()
    lo = pl.multiple_of(y * 32, 32)

    def pack(t, taken):
        col = src_ref[x * TILES + t] // 128
        shift = col * 8
        at = jnp.bitwise_and(lax.shift_right_logical(taken, shift), 255)
        send_ref[col, at] = adj[t, pl.ds(lo, 32), :]
        return taken + lax.shift_left(jnp.int32(1), shift)

    lax.fori_loop(0, TILES, pack, zero, unroll=4)

    def keep(j, _):
        t = list_ref[x * LIST + j] // TILES
        own_ref[j] = adj[t]
        return 0

    lax.fori_loop(0, counts_at(start_ref, x), keep, 0)


def counts_at(start_ref, x):
    return start_ref[x * 16 + R]


def pack(sources, adjacency):
    smem = pl.BlockSpec(memory_space=pltpu.SMEM)
    vmem = pl.BlockSpec(memory_space=pltpu.VMEM)
    return pl.pallas_call(
        pack_kernel,
        name="pack_tiles",
        out_shape=(
            jax.ShapeDtypeStruct((NX, CAP, 32, B), BF),
            jax.ShapeDtypeStruct((CAP, B, B), BF),
            jax.ShapeDtypeStruct((NX * LIST,), jnp.int32),
            jax.ShapeDtypeStruct((NX * 16,), jnp.int32),
        ),
        in_specs=[smem, pl.BlockSpec(memory_space=pl.ANY)],
        out_specs=(vmem, vmem, smem, smem),
        scratch_shapes=[pltpu.VMEM((TILES, B, B), BF), pltpu.SemaphoreType.DMA],
        compiler_params=pltpu.CompilerParams(vmem_limit_bytes=VMEM_LIMIT),
    )(sources, adjacency.reshape(TILES, B, B))


class Ring:
    def __init__(self, me, np_, own, gathered, sems):
        self.me, self.np, self.own, self.gathered = me, np_, own, gathered
        self.zs, self.zr, self.ss, self.sr = sems
        self.per = R // np_
        self.started = []

    @staticmethod
    def scratch(np_):
        n = 2 * 4 * np_
        return [
            pltpu.SemaphoreType.DMA((n,)),
            pltpu.SemaphoreType.DMA((n,)),
            pltpu.SemaphoreType.DMA((NZ * np_,)),
            pltpu.SemaphoreType.DMA((NZ * np_,)),
        ]

    def has(self, way, s, k):
        if s < 3:
            return True
        return s == 3 and (k < self.np // 2) == (way == 0)

    def spot(self, hops, sibling, k):
        zo = lax.rem(self.me.z + (NZ - hops), NZ)
        c = 1 - self.me.c if sibling else self.me.c
        return self.gathered.at[zo, c, pl.ds(k * self.per, self.per)]

    def z_copy(self, way, s, k):
        hops = s if way == 0 else -s
        i = (way * 4 + s) * self.np + k
        src = self.own(k) if s == 0 else self.spot(hops, False, k)
        return remote(
            src,
            self.spot(hops, False, k),
            self.zs.at[i],
            self.zr.at[i],
            self.me.at(dz=1 if way == 0 else -1),
        )

    def z_arrival(self, way, s, k):
        hops = s + 1 if way == 0 else -(s + 1)
        i = (way * 4 + s) * self.np + k
        spot = self.spot(hops, False, k)
        return remote(spot, spot, self.zs.at[i], self.zr.at[i], self.me.at(dz=-1 if way == 0 else 1))

    def rel(self, hops):
        return (hops + NZ) % NZ

    def sib_copy(self, hops, k):
        i = self.rel(hops) * self.np + k
        src = self.own(k) if hops == 0 else self.spot(hops, False, k)
        return remote(src, self.spot(hops, False, k), self.ss.at[i], self.sr.at[i], self.me.at(sibling=True))

    def sib_arrival(self, hops, k):
        i = self.rel(hops) * self.np + k
        spot = self.spot(hops, True, k)
        return remote(spot, spot, self.ss.at[i], self.sr.at[i], self.me.at(sibling=True))

    def start(self, copy):
        copy.start()
        self.started.append(copy)

    def send_own(self, k):
        for way in range(2):
            self.start(self.z_copy(way, 0, k))
        self.start(self.sib_copy(0, k))

    def arrive(self, s, k):
        for way in range(2):
            if not self.has(way, s, k):
                continue
            self.z_arrival(way, s, k).wait_recv()
            if self.has(way, s + 1, k):
                self.start(self.z_copy(way, s + 1, k))
            self.start(self.sib_copy(s + 1 if way == 0 else -(s + 1), k))

    def finish(self):
        for rel in range(NZ):
            for k in range(self.np):
                self.sib_arrival(rel, k).wait_recv()
        for copy in self.started:
            copy.wait_send()


def first_kernel(x_ref, send_ref, own_ref, gath_ref, tiles_ref, zs, zr, ss, sr, xs, xr, ys, yr, loc):
    me = Place()
    partners = [me.at(dz=1), me.at(dz=-1), me.at(sibling=True), me.at(dy=1), me.at(dy=-1)]
    partners += [me.at(dx=1), me.at(dx=-1), me.at(dx=2)]
    meet(partners, len(partners))

    np_ = 2
    ring = Ring(me, np_, lambda k: x_ref.at[pl.ds(k * (R // np_), R // np_)], gath_ref, (zs, zr, ss, sr))
    keep_x = pltpu.make_async_copy(x_ref, gath_ref.at[me.z, me.c], loc.at[0])
    keep_t = pltpu.make_async_copy(own_ref, tiles_ref.at[me.x], loc.at[1])
    for k in range(np_):
        ring.send_own(k)

    half = CAP // 2
    started = []

    def go(copy):
        copy.start()
        started.append(copy)

    def quarter(dx, dy, lo=0, n=CAP):
        x = lax.rem(me.x + (dx + NX), NX)
        y = lax.rem(me.y + (dy + NY), NY)
        return tiles_ref.at[x, pl.ds(lo, n), pl.ds(pl.multiple_of(y * 32, 32), 32), :]

    for i, dx in enumerate((1, -1, 2)):
        x_to = lax.rem(me.x + (dx + NX), NX)
        go(remote(send_ref.at[x_to], quarter(0, 0), xs.at[i], xr.at[i], me.at(dx=dx)))
    keep_x.start()
    keep_t.start()

    froms = (-1, 1, 2)

    def tiles_from_x(i):
        spot = quarter(froms[i], 0)
        remote(spot, spot, xs.at[i], xr.at[i], me.at(dx=froms[i])).wait_recv()
        go(remote(spot, spot, ys.at[i * 4], yr.at[i * 4], me.at(dy=1)))
        go(remote(spot, spot, ys.at[i * 4 + 1], yr.at[i * 4 + 1], me.at(dy=-1)))

    def tiles_from_y(i):
        for way, dy in ((0, -1), (1, 1)):
            spot = quarter(froms[i], dy)
            sem = i * 4 + way
            remote(spot, spot, ys.at[sem], yr.at[sem], me.at(dy=dy)).wait_recv()
            part = quarter(froms[i], dy, way * half, half)
            go(remote(part, part, ys.at[sem + 2], yr.at[sem + 2], me.at(dy=-dy)))

    def tiles_last(i):
        for way, dy in ((0, -1), (1, 1)):
            spot = quarter(froms[i], 2, way * half, half)
            sem = i * 4 + way + 2
            remote(spot, spot, ys.at[sem], yr.at[sem], me.at(dy=dy)).wait_recv()

    ring.arrive(0, 0)
    tiles_from_x(0)
    tiles_from_x(1)
    ring.arrive(0, 1)
    ring.arrive(1, 0)
    tiles_from_x(2)
    tiles_from_y(0)
    ring.arrive(1, 1)
    tiles_from_y(1)
    ring.arrive(2, 0)
    tiles_from_y(2)
    ring.arrive(2, 1)
    ring.arrive(3, 0)
    ring.arrive(3, 1)
    for i in range(3):
        tiles_last(i)
    ring.finish()
    for copy in started:
        copy.wait_send()
    keep_x.wait()
    keep_t.wait()


def first_exchange(blocks, send, own):
    hbm = pl.BlockSpec(memory_space=pl.ANY)
    return pl.pallas_call(
        first_kernel,
        name="exchange_tiles_and_features",
        out_shape=(
            jax.ShapeDtypeStruct((NZ, NC, R, B, COLS), BF),
            jax.ShapeDtypeStruct((NX, CAP, B, B), BF),
        ),
        in_specs=[hbm, hbm, hbm],
        out_specs=(hbm, hbm),
        scratch_shapes=[
            *Ring.scratch(2),
            pltpu.SemaphoreType.DMA((3,)),
            pltpu.SemaphoreType.DMA((3,)),
            pltpu.SemaphoreType.DMA((12,)),
            pltpu.SemaphoreType.DMA((12,)),
            pltpu.SemaphoreType.DMA((2,)),
        ],
        compiler_params=pltpu.CompilerParams(collective_id=0, has_side_effects=True),
    )(blocks, send, own)


def partial_kernel(list_ref, start_ref, tiles_ref, gath_ref, part_ref, own_ref, prod):
    p = pl.program_id(0)

    def one(j, _):
        s = jnp.bitwise_and(list_ref[p * LIST + j], 127)
        prod[j] = jnp.dot(tiles_ref[0, j], gath_ref[s], preferred_element_type=F32)
        return 0

    count = start_ref[p * 16 + R]
    lax.fori_loop(0, (count + 1) // 2, lambda i, _: one(2 * i + 1, one(2 * i, 0)), 0)
    mine = p == lax.axis_index("dom") // (NZ * NC)

    def row(r, _):
        total = lax.fori_loop(
            start_ref[p * 16 + r],
            start_ref[p * 16 + r + 1],
            lambda j, acc: acc + prod[j],
            jnp.zeros((B, COLS), F32),
        )
        at = pl.ds(pl.multiple_of(r * B, B), B)
        part_ref[0, at] = total.astype(BF)

        @pl.when(mine)
        def _():
            own_ref[at] = total

        return 0

    lax.fori_loop(0, R, row, 0)


def partial_sums(lists, starts, tiles, gathered):
    smem = pl.BlockSpec(memory_space=pltpu.SMEM)
    return pl.pallas_call(
        partial_kernel,
        name="partial_aggregate",
        grid=(NX,),
        out_shape=(
            jax.ShapeDtypeStruct((NX, ROWS, COLS), BF),
            jax.ShapeDtypeStruct((ROWS, COLS), F32),
        ),
        in_specs=[
            smem,
            smem,
            pl.BlockSpec((1, CAP, B, B), lambda p: (p, 0, 0, 0)),
            pl.BlockSpec((NZ * NC * R, B, COLS), lambda p: (0, 0, 0)),
        ],
        out_specs=(
            pl.BlockSpec((1, ROWS, COLS), lambda p: (p, 0, 0)),
            pl.BlockSpec((ROWS, COLS), lambda p: (0, 0)),
        ),
        scratch_shapes=[pltpu.VMEM((CAP, B, COLS), F32)],
        compiler_params=pltpu.CompilerParams(vmem_limit_bytes=VMEM_LIMIT),
    )(lists, starts, tiles, gathered.reshape(NZ * NC * R, B, COLS))


NCH = 4
RC = ROWS // NCH
HC = RC // 2


def finish_kernel(last, *refs):
    if last:
        part, own, weight, slots, where, out = refs[:6]
        refs = refs[6:]
    else:
        part, own, weight, gath_ref = refs[:4]
        refs = refs[4:]
    relay_in, relay_out, sums_in, agg, done, xs, xr, ys, yr = refs[:9]
    refs = refs[9:]
    me = Place()
    partners = [me.at(dx=1), me.at(dx=-1), me.at(dy=1), me.at(dy=-1)]
    if last:
        leave, came, ms, mr = refs
        partners += [me.ring(1), me.ring(-1)]
    else:
        loc = refs[4]
        partners += [me.at(dz=1), me.at(dz=-1), me.at(sibling=True)]
        ring = Ring(me, NCH, lambda k: done.at[pl.ds(k * (R // NCH), R // NCH)], gath_ref, refs[:4])
    meet(partners, len(partners))

    started = []

    def go(copy):
        copy.start()
        started.append(copy)

    ways = ((0, 1), (1, -1))
    side = lambda dx: lax.rem(me.x + (dx + NX), NX)
    halves = lambda k: (pl.ds(k * RC, HC), pl.ds(k * RC + HC, HC))

    def x_far(k):
        for way, d in ways:
            i = (way * NCH + k) * 3
            go(remote(part.at[side(2), halves(k)[way]], relay_in.at[way, k], xs.at[i], xr.at[i], me.at(dx=d)))

    def x_near(k):
        for way, d in ways:
            i = (way * NCH + k) * 3 + 1
            rows = halves(k)[1 - way]
            go(remote(part.at[side(d), rows], sums_in.at[way, rows], xs.at[i], xr.at[i], me.at(dx=d)))

    def x_relay(k):
        for way, d in ways:
            i = (way * NCH + k) * 3
            spot = relay_in.at[way, k]
            remote(spot, spot, xs.at[i], xr.at[i], me.at(dx=-d)).wait_recv()
            rows = halves(k)[way]
            mine = part[side(d), rows, :].astype(F32)
            relay_out[way, k] = (mine + relay_in[way, k].astype(F32)).astype(BF)
            go(remote(relay_out.at[way, k], sums_in.at[way, rows], xs.at[i + 2], xr.at[i + 2], me.at(dx=d)))

    def x_sum(k):
        for way, d in ways:
            for j, rows in ((1, halves(k)[1 - way]), (2, halves(k)[way])):
                i = (way * NCH + k) * 3 + j
                spot = sums_in.at[way, rows]
                remote(spot, spot, xs.at[i], xr.at[i], me.at(dx=-d)).wait_recv()
        rows = pl.ds(k * RC, RC)
        total = own[rows, :] + sums_in[0, rows, :].astype(F32) + sums_in[1, rows, :].astype(F32)
        agg[me.y, rows, :] = total.astype(BF)
        for way, d in ways:
            i = (way * NCH + k) * 2
            spot = agg.at[me.y, rows]
            go(remote(spot, spot, ys.at[i], yr.at[i], me.at(dy=d)))

    def y_pass(k):
        for way, d in ways:
            i = (way * NCH + k) * 2
            y_from = lax.rem(me.y + (NY - d), NY)
            spot = agg.at[y_from, pl.ds(k * RC, RC)]
            remote(spot, spot, ys.at[i], yr.at[i], me.at(dy=-d)).wait_recv()
            spot = agg.at[y_from, halves(k)[way]]
            go(remote(spot, spot, ys.at[i + 1], yr.at[i + 1], me.at(dy=d)))

    def transform(k):
        for way, d in ways:
            i = (way * NCH + k) * 2 + 1
            spot = agg.at[lax.rem(me.y + 2, NY), halves(k)[way]]
            remote(spot, spot, ys.at[i], yr.at[i], me.at(dy=-d)).wait_recv()
        rows = pl.ds(k * RC, RC)
        total = jnp.zeros((RC, COLS), F32)
        for y in range(NY):
            total += jnp.dot(agg[y, rows, :], weight[pl.ds(y * COLS, COLS), :], preferred_element_type=F32)
        if not last:
            total = jnp.maximum(total, 0.0)
        done[pl.ds(k * (R // NCH), R // NCH)] = total.astype(BF).reshape(R // NCH, B, COLS)
        if not last:
            ring.send_own(k)
            copy = pltpu.make_async_copy(
                done.at[pl.ds(k * (R // NCH), R // NCH)],
                gath_ref.at[me.z, me.c, pl.ds(k * (R // NCH), R // NCH)],
                loc.at[k],
            )
            copy.start()
            kept.append(copy)

    kept = []
    x_far(0)
    for slot in range(NCH + 3):
        if slot + 1 < NCH:
            x_far(slot + 1)
        if slot < NCH:
            x_near(slot)
            x_relay(slot)
        if 0 <= slot - 1 < NCH:
            x_sum(slot - 1)
        if 0 <= slot - 2 < NCH:
            y_pass(slot - 2)
        if 0 <= slot - 3 < NCH:
            transform(slot - 3)
        if not last:
            for s in range(4):
                k = slot - 4 - s
                if 0 <= k < NCH:
                    ring.arrive(s, k)
    if last:
        for m in range(2):
            leave[m] = done[slots[m]]
        move = remote(leave, came, ms, mr, me.ring(1))
        move.start()
        move.wait()
        done[pl.ds(R, 2)] = came[...]
        for r in range(R):
            out[pl.ds(r * B, B), :] = done[where[r]]
    else:
        for slot in range(NCH + 3, NCH + 3 + 8):
            for s in range(4):
                k = slot - 4 - s
                if 0 <= k < NCH:
                    ring.arrive(s, k)
        ring.finish()
        for copy in kept:
            copy.wait()
    for copy in started:
        copy.wait_send()


def finish(last, part, own, weight, slots=None, where=None):
    vmem = pl.BlockSpec(memory_space=pltpu.VMEM)
    smem = pl.BlockSpec(memory_space=pltpu.SMEM)
    scratch = [
        pltpu.VMEM((2, NCH, HC, COLS), BF),
        pltpu.VMEM((2, NCH, HC, COLS), BF),
        pltpu.VMEM((2, ROWS, COLS), BF),
        pltpu.VMEM((NY, ROWS, COLS), BF),
        pltpu.VMEM((R + 2, B, COLS), BF),
        pltpu.SemaphoreType.DMA((2 * NCH * 3,)),
        pltpu.SemaphoreType.DMA((2 * NCH * 3,)),
        pltpu.SemaphoreType.DMA((2 * NCH * 2,)),
        pltpu.SemaphoreType.DMA((2 * NCH * 2,)),
    ]
    if last:
        scratch += [pltpu.VMEM((2, B, COLS), BF), pltpu.VMEM((2, B, COLS), BF), pltpu.SemaphoreType.DMA, pltpu.SemaphoreType.DMA]
        out_shape = jax.ShapeDtypeStruct((ROWS, COLS), BF)
        out_spec = vmem
        args, in_specs = (part, own, weight, slots, where), [vmem, vmem, vmem, smem, smem]
    else:
        scratch += [*Ring.scratch(NCH), pltpu.SemaphoreType.DMA((NCH,))]
        out_shape = jax.ShapeDtypeStruct((NZ, NC, R, B, COLS), BF)
        out_spec = pl.BlockSpec(memory_space=pl.ANY)
        args, in_specs = (part, own, weight), [vmem, vmem, vmem]
    return pl.pallas_call(
        functools.partial(finish_kernel, last),
        name="layer_two_end" if last else "layer_one_end",
        out_shape=out_shape,
        in_specs=in_specs,
        out_specs=out_spec,
        scratch_shapes=scratch,
        compiler_params=pltpu.CompilerParams(
            collective_id=2 if last else 1, has_side_effects=True, vmem_limit_bytes=VMEM_LIMIT
        ),
    )(*args)


def on_device(features, adjacency, tile_src, mig_slot, weight_one, weight_two):
    dom = lax.axis_index("dom")
    z, c = lax.rem(dom // NC, NZ), lax.rem(dom, NC)
    grid = tile_src.reshape(NX, NZ, NC, TILES)
    sources = lax.dynamic_slice(grid, (0, z, c, 0), (NX, 1, 1, TILES)).reshape(NX * TILES)
    slots = lax.dynamic_slice_in_dim(mig_slot, dom, 1, 0).reshape(2)
    spot = jnp.arange(R, dtype=jnp.int32)
    where = jnp.where(spot == slots[0], R, jnp.where(spot == slots[1], R + 1, spot))
    col = lax.axis_index("feat") * COLS
    w_one = lax.dynamic_slice_in_dim(weight_one, col, COLS, 1)
    w_two = lax.dynamic_slice_in_dim(weight_two, col, COLS, 1)

    send, own, lists, starts = pack(sources, adjacency)
    gathered, tiles = first_exchange(features.reshape(R, B, COLS), send, own)
    part, mine = partial_sums(lists, starts, tiles, gathered)
    gathered = finish(False, part, mine, w_one)
    part, mine = partial_sums(lists, starts, tiles, gathered)
    return finish(True, part, mine, w_two, slots, where)


def solution(mesh):
    in_specs = (P("dom", "feat"), P("dom", None, None, None), P(), P(), P(), P())
    return jax.shard_map(
        on_device, mesh=mesh, in_specs=in_specs, out_specs=P("dom", "feat"), check_vma=False
    )
```

time: 618 us -> 226 us (0.37)
  waiting for transfers between devices: 388 us -> 0 us
  Pallas kernels: 0 us -> 216 us
  local copies, waits for them, and re-layouts: 121 us -> 7.69 us
  blocking collectives: 30.4 us -> 0 us
  starting transfers between devices: 29.5 us -> 0 us
  other arithmetic: 27.4 us -> 1.81 us
  matrix products: 18.3 us -> 0 us
    all_to_all x4 -> x0, waiting for transfers between devices: 372 us -> none  [the longest x2 360 us: aggregate(): lax.all_to_all(outgoing, 'dom', split_axis=0, concat_axis=0, tiled=True)]
    pallas_call x0 -> x6, Pallas kernels: none -> 216 us  [the longest x2 113 us: finish(): pl.pallas_call(functools.partial(finish_kernel, last), name='layer_two_en...]
    gather x11 -> x0, local copies, waits for them, and re-layouts: 96.7 us -> none  [the longest x1 28 us: place_blocks(): marked = jnp.take(mig_slot, holders, axis=0)]
    all_to_all x1 -> x0, blocking collectives: 30.4 us -> none  [copy_for_each(): lax.all_to_all(jnp.broadcast_to(value[None], (count, *value.shape)), axis...]
    all_to_all x4 -> x0, starting transfers between devices: 28.8 us -> none  [the longest x2 18.3 us: aggregate(): lax.all_to_all(outgoing, 'dom', split_axis=0, concat_axis=0, tiled=True)]
    dot_general x6 -> x0, matrix products: 18.3 us -> none  [the longest x2 12.1 us: aggregate(): jnp.einsum('rtij,rtjf->rif', adjacency, sources, preferred_element_type=j...]
    ppermute x2 -> x0, waiting for transfers between devices: 16 us -> none  [from_behind(): lax.ppermute(value, axis, [(i, (i + by) % count) for i in range(count)])]
    concatenate x4 -> x0, other arithmetic: 15.8 us -> none  [the longest x2 15.1 us: aggregate(): jnp.concatenate([local_blocks, arrived.reshape(-1, B, col_width)], axis=0)]
  transfers between devices with their start and end apart: 6 -> 0, of which waited for: 5 -> 0; matrix products, arithmetic and copies ran while one was open for 4% -> 0% of each run, Pallas kernels for 0% -> 0%
where the time goes in v1:
time: 226 us
  Pallas kernels  216 us (96%)
  local copies, waits for them, and re-layouts  7.69 us (3%)
    pallas_call x2, Pallas kernels, finish(): pl.pallas_call(functools.partial(finish_kernel, last), name='layer_two_en...  113 us
    pallas_call x1, Pallas kernels, first_exchange(): pl.pallas_call(first_kernel, name='exchange_tiles_and_features', out_shap...  57.6 us
    pallas_call x2, Pallas kernels, partial_sums(): pl.pallas_call(partial_kernel, name='partial_aggregate', grid=(NX,), out_...  37.3 us
    pallas_call x1, Pallas kernels, pack(): pl.pallas_call(pack_kernel, name='pack_tiles', out_shape=(jax.ShapeDtypeS...  7.74 us

profile of v1, /device:TPU:8, one launch (start us, length us, event | category | flops | bytes accessed | tf_op | source)
XLA Modules:
  0.0 225.6 jit_solution(6289157593931136263)
XLA Ops:
  0.0 1.4 fusion
  1.4 0.5 fusion.1
  2.0 1.8 compare_select_fusion.1.refs_4_
  3.8 0.9 copy.7
  4.7 0.1 reshape.25
  4.8 0.6 constant_dynamic-slice_fusion.3
  5.4 2.2 constant_dynamic-slice_fusion.1
  7.6 7.7 %pack_tiles.1 = (bf16[4,34,32,128]{3,2,1,0:T(8,128)(2,1)}, bf16[34,128,128]{2,1,0:T(8,128)(2,1)}, s32[192]{0:T(256)}, s32[64]{0:T(128)}) custom-call(s32[512]{0:T(512)} %bitcast.11, bf16[128,128,128]{2,1,0:T(8,128)(2,1)} %bitcast.9), custom_call_target="tpu_custom_call" | custom-call | tf_op jit(solution)/shard_map/pack_tiles/pallas_call | solution.py:111
  15.4 57.6 %exchange_tiles_and_features.1 = (bf16[8,2,8,128,256]{4,3,2,1,0:T(8,128)(2,1)}, bf16[4,34,128,128]{3,2,1,0:T(8,128)(2,1)}) custom-call(bf16[8,128,256]{2,1,0:T(8,128)(2,1)} %bitcast.10, bf16[4,34,32,128]{3,2,1,0:T(8,128)(2,1)} %get-tuple-element.17.send_ref, bf16[34,128,128]{2,1,0:T(8,128)(2,1)} %get-tuple-element.18.own_ref), custom_call_target="tpu_custom_call" | custom-call | tf_op jit(solution)/shard_map/exchange_tiles_and_features/pallas_call | solution.py:289
  73.0 18.6 %partial_aggregate.2 = (bf16[4,1024,256]{2,1,0:T(8,128)(2,1)}, f32[1024,256]{1,0:T(8,128)}) custom-call(s32[192]{0:T(256)} %get-tuple-element.15.list_ref, s32[64]{0:T(128)} %get-tuple-element.16.start_ref, bf16[4,34,128,128]{3,2,1,0:T(8,128)(2,1)} %get-tuple-element.19.tiles_ref, bf16[128,128,256]{2,1,0:T(8,128)(2,1)} %bitcast.8), custom_call_target="tpu_custom_call" | custom-call | tf_op jit(solution)/shard_map/partial_aggregate/pallas_call | solution.py:343
  91.7 73.5 %layer_one_end.1 = bf16[8,2,8,128,256]{4,3,2,1,0:T(8,128)(2,1)} custom-call(bf16[4,1024,256]{2,1,0:T(8,128)(2,1)} %get-tuple-element.21.refs_0_, f32[1024,256]{1,0:T(8,128)} %get-tuple-element.22.refs_1_, bf16[1024,256]{1,0:T(8,128)(2,1)} %get-tuple-element.30.refs_2_), custom_call_target="tpu_custom_call" | custom-call | tf_op jit(solution)/shard_map/layer_one_end/pallas_call | solution.py:532
  165.2 18.6 %partial_aggregate.3 = (bf16[4,1024,256]{2,1,0:T(8,128)(2,1)}, f32[1024,256]{1,0:T(8,128)}) custom-call(s32[192]{0:T(256)} %get-tuple-element.15.list_ref, s32[64]{0:T(128)} %get-tuple-element.16.start_ref, bf16[4,34,128,128]{3,2,1,0:T(8,128)(2,1)} %get-tuple-element.19.tiles_ref, bf16[128,128,256]{2,1,0:T(8,128)(2,1)} %bitcast.7), custom_call_target="tpu_custom_call" | custom-call | tf_op jit(solution)/shard_map/partial_aggregate/pallas_call | solution.py:343
  183.8 39.9 %layer_two_end.1 = bf16[1024,256]{1,0:T(8,128)(2,1)} custom-call(bf16[4,1024,256]{2,1,0:T(8,128)(2,1)} %get-tuple-element.23.refs_0_, f32[1024,256]{1,0:T(8,128)} %get-tuple-element.24.refs_1_, bf16[1024,256]{1,0:T(8,128)(2,1)} %get-tuple-element.29.refs_2_, s32[2]{0:T(128)} %get-tuple-element.25.refs_3_, s32[8]{0:T(128)} %compare_select_fusion.1.refs_4_), custom_call_target="tpu_custom_call" | custom-call | tf_op jit(solution)/shard_map/layer_two_end/pallas_call | solution.py:532
  223.7 1.9 copy.9

commit v2 on v0

v2 whole, which is shorter than its diff:
```python
import functools

import jax
import jax.numpy as jnp
from jax import lax
from jax.experimental import pallas as pl
from jax.experimental.pallas import tpu as pltpu
from jax.sharding import PartitionSpec as P

B = 128
R = 8
TPB = 16
NX, NZ, NC, NY = 4, 8, 2, 4
NDOM = NX * NZ * NC
COLS = 256
ROWS = R * B
TILES = R * TPB
PAIRS = NZ * NC + 1
SLOTS = 2 * PAIRS
QROWS = B // NY
NP = 4
RC = ROWS // NP
HC = RC // 2
PER = R // NP
MESH = pl.DeviceIdType.MESH
BF, F32 = jnp.bfloat16, jnp.float32
WAYS = ((0, 1), (1, -1))


class Place:
    def __init__(self):
        d = lax.axis_index("dom")
        self.dom = d
        self.y = lax.axis_index("feat")
        self.x = d // (NZ * NC)
        self.z = lax.rem(d // NC, NZ)
        self.c = lax.rem(d, NC)

    def at(self, dx=0, dz=0, sibling=False, dy=0):
        x = lax.rem(self.x + (dx + NX), NX)
        z = lax.rem(self.z + (dz + NZ), NZ)
        c = 1 - self.c if sibling else self.c
        y = lax.rem(self.y + (dy + NY), NY)
        return ((x * NZ + z) * NC + c, y)

    def along(self, by):
        return (lax.rem(self.dom + (by + NDOM), NDOM), self.y)

    def y_of(self, dy):
        return lax.rem(self.y + (dy + NY), NY)


def remote(src, dst, send, recv, device):
    return pltpu.make_async_remote_copy(
        src_ref=src, dst_ref=dst, send_sem=send, recv_sem=recv, device_id=device, device_id_type=MESH
    )


def table_kernel(src_ref, tab_ref):
    x = lax.axis_index("dom") // (NZ * NC)
    t_row = lax.broadcasted_iota(jnp.int32, (1, TILES), 1)
    earlier = lax.broadcasted_iota(jnp.int32, (TILES, TILES), 0) < lax.broadcasted_iota(jnp.int32, (TILES, TILES), 1)
    lane = lax.broadcasted_iota(jnp.int32, (40, 128), 1)
    slot = lax.broadcasted_iota(jnp.int32, (40, TILES), 0)
    total = jnp.zeros((40, 128), F32)

    def ranks(i):
        s = src_ref[pl.ds(lax.rem(x + i, NX), 1), :]
        q = lax.shift_right_logical(s, 3)
        down = jnp.transpose(jnp.broadcast_to(q, (TILES, TILES)))
        same = jnp.where(jnp.logical_and(down == q, earlier), 1.0, 0.0)
        return s, q, jnp.sum(same, axis=0, keepdims=True)

    def column(total, at, s, q, rank, col):
        here = lax.shift_right_logical(q, 4) == col
        regular = jnp.logical_and(here, rank < 1.5)
        more = jnp.logical_and(here, rank > 1.5)
        first = jnp.min(jnp.where(more, t_row, TILES), axis=1, keepdims=True)
        place = jnp.where(
            regular,
            2 * jnp.bitwise_and(q, 15) + rank.astype(jnp.int32),
            jnp.where(more, SLOTS - 2 + jnp.where(t_row > first, 1, 0), -1),
        )
        entry = (1 + t_row * 128 + jnp.bitwise_and(s, 127)).astype(F32)
        found = jnp.sum(jnp.where(slot == place, entry, 0.0), axis=1, keepdims=True)
        return total + jnp.where(lane == at, found, 0.0)

    own = ranks(0)
    for i in range(NX):
        total = column(total, i, *(own if i == 0 else ranks(i)), x)
        total = column(total, NX + i, *own, lax.rem(x + i, NX))
    tab_ref[...] = total.astype(jnp.int32)


def tables(sources):
    vmem = pl.BlockSpec(memory_space=pltpu.VMEM)
    return pl.pallas_call(
        table_kernel,
        name="tile_tables",
        out_shape=jax.ShapeDtypeStruct((40, 128), jnp.int32),
        in_specs=[vmem],
        out_specs=vmem,
    )(sources)


def ring_scratch():
    n = 2 * 4 * NP
    return [pltpu.SemaphoreType.DMA((n,)), pltpu.SemaphoreType.DMA((n,))] + [
        pltpu.SemaphoreType.DMA((NZ * NP,)),
        pltpu.SemaphoreType.DMA((NZ * NP,)),
    ]


def end_scratch():
    return [
        pltpu.VMEM((NX, ROWS, COLS), BF),
        pltpu.VMEM((2, NP, HC, COLS), BF),
        pltpu.VMEM((2, NP, HC, COLS), BF),
        pltpu.VMEM((2, ROWS, COLS), BF),
        pltpu.VMEM((NY, ROWS, COLS), BF),
        pltpu.SemaphoreType.DMA((2 * NP * 3,)),
        pltpu.SemaphoreType.DMA((2 * NP * 3,)),
        pltpu.SemaphoreType.DMA((2 * NP * 2,)),
        pltpu.SemaphoreType.DMA((2 * NP * 2,)),
    ]


class Ring:
    def __init__(self, me, blocks, own, sems):
        self.me, self.blocks, self.own = me, blocks, own
        self.zs, self.zr, self.ss, self.sr = sems

    def spot(self, hops, side, k):
        return self.blocks[hops % NZ][side].at[pl.ds(k * PER, PER)]

    def source(self, hops, k):
        return self.own(k) if hops % NZ == 0 else self.spot(hops, 0, k)

    def z_copy(self, way, s, k):
        hops = s if way == 0 else -s
        on = s + 1 if way == 0 else -(s + 1)
        i = (way * 4 + s) * NP + k
        up = 1 if way == 0 else -1
        return remote(self.source(hops, k), self.spot(on, 0, k), self.zs.at[i], self.zr.at[i], self.me.at(dz=up))

    def z_arrival(self, way, s, k):
        spot = self.spot(s + 1 if way == 0 else -(s + 1), 0, k)
        i = (way * 4 + s) * NP + k
        return remote(spot, spot, self.zs.at[i], self.zr.at[i], self.me.at(dz=-1 if way == 0 else 1))

    def sib_copy(self, hops, k):
        i = (hops % NZ) * NP + k
        return remote(
            self.source(hops, k), self.spot(hops, 1, k), self.ss.at[i], self.sr.at[i], self.me.at(sibling=True)
        )

    def sib_arrival(self, hops, k):
        i = (hops % NZ) * NP + k
        spot = self.spot(hops, 1, k)
        return remote(spot, spot, self.ss.at[i], self.sr.at[i], self.me.at(sibling=True))

    def send_own(self, k):
        for way in range(2):
            self.z_copy(way, 0, k).start()
        self.sib_copy(0, k).start()

    def arrive(self, way, s, k, on):
        self.z_arrival(way, s, k).wait_recv()
        if on:
            self.z_copy(way, s + 1, k).start()
        self.sib_copy(s + 1 if way == 0 else -(s + 1), k).start()

    def from_sibling(self, *hops):
        for h in hops:
            for k in range(NP):
                self.sib_arrival(h, k).wait_recv()

    def finish(self):
        for way in range(2):
            for s in range(4):
                for k in range(NP):
                    if s < 3 or (k < NP // 2) == (way == 0):
                        self.z_copy(way, s, k).wait_send()
        for h in range(NZ):
            for k in range(NP):
                self.sib_copy(h, k).wait_send()

    def run(self, between):
        for s in range(4):
            if s:
                self.from_sibling(*sorted({(s - 1) % NZ, -(s - 1) % NZ}))

            def turn(k, _, ways=(0, 1), s=s):
                for way in ways:
                    self.arrive(way, s, k, s < 2)
                if s:
                    between(s - 1, k)
                return 0

            if s < 2:
                lax.fori_loop(0, NP, turn, 0)
            elif s == 2:

                def third(k, _, way=0):
                    for w in range(2):
                        self.arrive(w, 2, k, w == way)
                    between(1, k)
                    return 0

                lax.fori_loop(0, NP // 2, third, 0)
                lax.fori_loop(NP // 2, NP, functools.partial(third, way=1), 0)
            else:
                lax.fori_loop(0, NP // 2, functools.partial(turn, ways=(0,)), 0)
                lax.fori_loop(NP // 2, NP, functools.partial(turn, ways=(1,)), 0)
        self.from_sibling(3, -3 % NZ)
        self.from_sibling(4)


STEPS = (
    ((0, 0), (0, 1)),
    ((1, 0), (1, 1), (7, 0), (7, 1)),
    ((2, 0), (2, 1), (6, 0), (6, 1)),
    ((3, 0), (3, 1), (5, 0), (5, 1)),
    ((4, 0), (4, 1)),
)


def whole_kernel(tab, mig, x_ref, adj_ref, w1_ref, w2_ref, out, *refs):
    refs = list(refs)

    def take(n):
        head = refs[:n]
        del refs[:n]
        return head

    flat = [take(2 * NZ) for _ in range(2)]
    blocks = [[f[2 * h : 2 * h + 2] for h in range(NZ)] for f in flat]
    adj, tiles, send, w1, w2, acc, lhs, rhs, done, leave, came = take(11)
    loc, xs, xr, ys, yr, ms, mr = take(7)
    ring_sems = [take(4) for _ in range(2)]
    ends = [take(9) for _ in range(2)]
    me = Place()

    col = pl.ds(pl.multiple_of(me.y * COLS, COLS), COLS)
    loads = [
        pltpu.make_async_copy(adj_ref, adj, loc.at[0]),
        pltpu.make_async_copy(x_ref, blocks[0][0][0], loc.at[1]),
        pltpu.make_async_copy(w1_ref.at[:, col], w1, loc.at[2]),
        pltpu.make_async_copy(w2_ref.at[:, col], w2, loc.at[3]),
    ]
    for load in loads:
        load.start()

    partners = [me.at(dz=1), me.at(dz=-1), me.at(sibling=True), me.at(dy=1), me.at(dy=-1)]
    partners += [me.at(dx=1), me.at(dx=-1), me.at(dx=2), me.along(1), me.along(-1)]
    barrier = pltpu.get_barrier_semaphore()
    for p in partners:
        pl.semaphore_signal(barrier, inc=1, device_id=p, device_id_type=MESH)
    pl.semaphore_wait(barrier, len(partners))

    rings = [
        Ring(me, blocks[0], lambda k: x_ref.at[pl.ds(k * PER, PER)], ring_sems[0]),
        Ring(me, blocks[1], lambda k: blocks[1][0][0].at[pl.ds(k * PER, PER)], ring_sems[1]),
    ]
    for k in range(NP):
        rings[0].send_own(k)

    started = []

    def go(copy):
        copy.start()
        started.append(copy)

    q_rows = lambda dy: pl.ds(pl.multiple_of(me.y_of(dy) * QROWS, QROWS), QROWS)
    loads[0].wait()

    def found(j, column):
        entry = tab[j, column]
        return entry, lax.shift_right_logical(jnp.maximum(entry - 1, 0), 7)

    def pack(i, dx, j, _):
        for k in range(2):
            entry, t = found(2 * j + k, NX + dx % NX)
            part = adj[t, q_rows(0), :]
            send[i, j, :, k * B : (k + 1) * B] = jnp.where(entry > 0, part, jnp.zeros_like(part))
        return 0

    def keep(j, _):
        for k in range(2):
            entry, t = found(2 * j + k, NX)
            part = adj[t]
            tiles[0, j, :, k * B : (k + 1) * B] = jnp.where(entry > 0, part, jnp.zeros_like(part))
        return 0

    def quarter(i, dy, lo=0, n=PAIRS):
        return tiles.at[i, pl.ds(lo, n), q_rows(dy), :]

    hops_x = (1, -1, 2)
    for i, dx in enumerate(hops_x):
        lax.fori_loop(0, PAIRS, functools.partial(pack, i, dx), 0)
        go(remote(send.at[i], quarter(-dx % NX, 0), xs.at[i], xr.at[i], me.at(dx=dx)))

    half = (PAIRS + 1) // 2
    cut = ((0, half), (half, PAIRS - half))

    def tiles_from_x(i):
        dx = hops_x[i]
        spot = quarter(-dx % NX, 0)
        remote(spot, spot, xs.at[i], xr.at[i], me.at(dx=-dx)).wait_recv()
        for way, d in WAYS:
            go(remote(spot, spot, ys.at[i * 4 + way], yr.at[i * 4 + way], me.at(dy=d)))

    def tiles_from_y(i):
        for way, d in WAYS:
            spot = quarter(-hops_x[i] % NX, -d)
            sem = i * 4 + way
            remote(spot, spot, ys.at[sem], yr.at[sem], me.at(dy=-d)).wait_recv()
            part = quarter(-hops_x[i] % NX, -d, *cut[way])
            go(remote(part, part, ys.at[sem + 2], yr.at[sem + 2], me.at(dy=d)))

    def tiles_last(i):
        for way, d in WAYS:
            spot = quarter(-hops_x[i] % NX, 2, *cut[way])
            sem = i * 4 + way + 2
            remote(spot, spot, ys.at[sem], yr.at[sem], me.at(dy=-d)).wait_recv()

    def place_of(hops, side):
        z = lax.rem(me.z + (NZ - hops), NZ)
        return z * NC + (1 - me.c if side else me.c)

    def spread(i, rd, pair):
        rows = []
        for k in range(2):
            entry = jnp.maximum(tab[2 * pair + k, rd] - 1, 0)
            tile = tiles[rd, pair, :, k * B : (k + 1) * B]
            at = pl.ds((2 * i + k) * B, B)
            r = lax.shift_right_logical(entry, 11)
            for row in range(R):
                lhs[row * B : (row + 1) * B, at] = jnp.where(r == row, tile, jnp.zeros_like(tile))
            rows.append((jnp.bitwise_and(entry, 127), at))
        return rows

    def product(layer, step, rd):
        held = blocks[layer]
        for i, (hops, side) in enumerate(STEPS[step]):
            for entry, at in spread(i, rd, place_of(hops, side)):
                rhs[at, :] = held[hops][side][jnp.bitwise_and(entry, 7)]
        n = len(STEPS[step])
        if step == 4:
            for entry, at in spread(n, rd, PAIRS - 1):
                b, q = jnp.bitwise_and(entry, 7), lax.shift_right_logical(entry, 3)
                got = held[0][0][b]
                for hops in range(NZ):
                    for side in range(2):
                        if hops or side:
                            got = jnp.where(q == place_of(hops, side), held[hops][side][b], got)
                rhs[at, :] = got
            n += 1
        width = n * 2 * B
        total = jnp.dot(lhs[:, :width], rhs[:width, :], preferred_element_type=F32)
        acc[rd] = total if step == 0 else acc[rd] + total

    def layer_end(layer, weight, put):
        part, relay_in, relay_out, sums_in, agg, xs, xr, ys, yr = ends[layer]
        halves = lambda k: (pl.ds(k * RC, HC), pl.ds(k * RC + HC, HC))

        def x_far(k):
            rows = pl.ds(k * RC, RC)
            part[2, rows, :] = acc[2, rows, :].astype(BF)
            for way, d in WAYS:
                i = (way * NP + k) * 3
                go(remote(part.at[2, halves(k)[way]], relay_in.at[way, k], xs.at[i], xr.at[i], me.at(dx=d)))

        def x_near(k):
            for way, d in WAYS:
                i = (way * NP + k) * 3 + 1
                rows = halves(k)[1 - way]
                part[d % NX, rows, :] = acc[d % NX, rows, :].astype(BF)
                go(remote(part.at[d % NX, rows], sums_in.at[way, rows], xs.at[i], xr.at[i], me.at(dx=d)))

        def x_relay(k):
            for way, d in WAYS:
                i = (way * NP + k) * 3
                spot = relay_in.at[way, k]
                remote(spot, spot, xs.at[i], xr.at[i], me.at(dx=-d)).wait_recv()
                rows = halves(k)[way]
                relay_out[way, k] = (acc[d % NX, rows, :] + relay_in[way, k].astype(F32)).astype(BF)
                go(remote(relay_out.at[way, k], sums_in.at[way, rows], xs.at[i + 2], xr.at[i + 2], me.at(dx=d)))

        def x_sum(k):
            for way, d in WAYS:
                for j, rows in ((1, halves(k)[1 - way]), (2, halves(k)[way])):
                    i = (way * NP + k) * 3 + j
                    spot = sums_in.at[way, rows]
                    remote(spot, spot, xs.at[i], xr.at[i], me.at(dx=-d)).wait_recv()
            rows = pl.ds(k * RC, RC)
            total = acc[0, rows, :] + sums_in[0, rows, :].astype(F32) + sums_in[1, rows, :].astype(F32)
            agg[me.y, rows, :] = total.astype(BF)
            for way, d in WAYS:
                i = (way * NP + k) * 2
                spot = agg.at[me.y, rows]
                go(remote(spot, spot, ys.at[i], yr.at[i], me.at(dy=d)))

        def y_pass(k):
            for way, d in WAYS:
                i = (way * NP + k) * 2
                spot = agg.at[me.y_of(-d), pl.ds(k * RC, RC)]
                remote(spot, spot, ys.at[i], yr.at[i], me.at(dy=-d)).wait_recv()
                spot = agg.at[me.y_of(-d), halves(k)[way]]
                go(remote(spot, spot, ys.at[i + 1], yr.at[i + 1], me.at(dy=d)))

        def transform(k):
            for way, d in WAYS:
                i = (way * NP + k) * 2 + 1
                spot = agg.at[me.y_of(2), halves(k)[way]]
                remote(spot, spot, ys.at[i], yr.at[i], me.at(dy=-d)).wait_recv()
            total = jnp.zeros((RC, COLS), F32)
            for y in range(NY):
                total += jnp.dot(
                    agg[y, pl.ds(k * RC, RC), :], weight[pl.ds(y * COLS, COLS), :], preferred_element_type=F32
                )
            put(k, total)

        x_far(0)
        for turn in range(NP + 3):
            if turn + 1 < NP:
                x_far(turn + 1)
            if turn < NP:
                x_near(turn)
                x_relay(turn)
            if 0 <= turn - 1 < NP:
                x_sum(turn - 1)
            if 0 <= turn - 2 < NP:
                y_pass(turn - 2)
            if 0 <= turn - 3 < NP:
                transform(turn - 3)

    first = rings[0]
    both = lambda s, k: [first.arrive(way, s, k, s < 2 or (s == 2 and (k < NP // 2) == (way == 0))) for way in range(2)]
    lax.fori_loop(0, PAIRS, keep, 0)
    both(0, 0)
    both(0, 1)
    tiles_from_x(0)
    tiles_from_x(1)
    both(0, 2)
    both(0, 3)
    tiles_from_x(2)
    both(1, 0)
    both(1, 1)
    tiles_from_y(0)
    both(1, 2)
    both(1, 3)
    tiles_from_y(1)
    both(2, 0)
    both(2, 1)
    tiles_from_y(2)
    both(2, 2)
    both(2, 3)
    loads[1].wait()
    for k in range(NP):
        first.arrive(0 if k < NP // 2 else 1, 3, k, False)
    for i in range(3):
        tiles_last(i)

    def layer_one(rd, _):
        for step in range(4):
            product(0, step, rd)
        return 0

    first.from_sibling(*(h for h in range(NZ) if h != 4))
    lax.fori_loop(0, NX, layer_one, 0)
    first.from_sibling(4)
    lax.fori_loop(0, NX, lambda rd, _: product(0, 4, rd) or 0, 0)
    loads[2].wait()
    loads[3].wait()
    second = rings[1]

    def put_hidden(k, total):
        hidden = jnp.maximum(total, 0.0).astype(BF).reshape(PER, B, COLS)
        blocks[1][0][0][pl.ds(k * PER, PER)] = hidden
        second.send_own(k)

    layer_end(0, w1, put_hidden)

    second.run(lambda step, k: product(1, step, k))

    def layer_two(rd, _):
        product(1, 3, rd)
        product(1, 4, rd)
        return 0

    lax.fori_loop(0, NX, layer_two, 0)

    def put_out(k, total):
        done[pl.ds(k * PER, PER)] = total.astype(BF).reshape(PER, B, COLS)

    layer_end(1, w2, put_out)

    slots = [mig[m, me.dom] for m in range(2)]
    for m in range(2):
        leave[m] = done[slots[m]]
    move = remote(leave, came, ms, mr, me.along(1))
    move.start()
    move.wait()
    done[pl.ds(R, 2)] = came[...]
    for r in range(R):
        at = jnp.where(slots[0] == r, R, jnp.where(slots[1] == r, R + 1, r))
        out[pl.ds(r * B, B), :] = done[at]
    for ring in rings:
        ring.finish()
    for copy in started:
        copy.wait_send()


def run_all(tab, mig_slot, features, adjacency, weight_one, weight_two):
    vmem = pl.BlockSpec(memory_space=pltpu.VMEM)
    smem = pl.BlockSpec(memory_space=pltpu.SMEM)
    hbm = pl.BlockSpec(memory_space=pl.ANY)
    dma = pltpu.SemaphoreType.DMA
    return pl.pallas_call(
        whole_kernel,
        name="two_layers",
        out_shape=jax.ShapeDtypeStruct((ROWS, COLS), BF),
        in_specs=[smem, smem, hbm, hbm, hbm, hbm],
        out_specs=vmem,
        scratch_shapes=[pltpu.VMEM((R, B, COLS), BF)] * (4 * NZ)
        + [
            pltpu.VMEM((TILES, B, B), BF),
            pltpu.VMEM((NX, PAIRS, B, 2 * B), BF),
            pltpu.VMEM((3, PAIRS, QROWS, 2 * B), BF),
            pltpu.VMEM((NY * COLS, COLS), BF),
            pltpu.VMEM((NY * COLS, COLS), BF),
            pltpu.VMEM((NX, ROWS, COLS), F32),
            pltpu.VMEM((ROWS, 8 * B), BF),
            pltpu.VMEM((8 * B, COLS), BF),
            pltpu.VMEM((R + 2, B, COLS), BF),
            pltpu.VMEM((2, B, COLS), BF),
            pltpu.VMEM((2, B, COLS), BF),
            dma((4,)),
            dma((3,)),
            dma((3,)),
            dma((12,)),
            dma((12,)),
            dma,
            dma,
        ]
        + ring_scratch() * 2
        + end_scratch() * 2,
        compiler_params=pltpu.CompilerParams(
            collective_id=0, has_side_effects=True, vmem_limit_bytes=60 * 1024 * 1024
        ),
    )(tab, mig_slot.T, features, adjacency, weight_one, weight_two)


def on_device(features, adjacency, tile_src, mig_slot, weight_one, weight_two):
    dom = lax.axis_index("dom")
    z, c = lax.rem(lax.div(dom, NC), NZ), lax.rem(dom, NC)
    grid = tile_src.reshape(NX, NZ, NC, TILES)
    sources = lax.dynamic_slice(grid, (0, z, c, 0), (NX, 1, 1, TILES)).reshape(NX, TILES)
    tab = tables(sources)
    return run_all(
        tab, mig_slot, features.reshape(R, B, COLS), adjacency.reshape(TILES, B, B), weight_one, weight_two
    )


def solution(mesh):
    in_specs = (P("dom", "feat"), P("dom", None, None, None), P(), P(), P(), P())
    return jax.shard_map(
        on_device, mesh=mesh, in_specs=in_specs, out_specs=P("dom", "feat"), check_vma=False
    )
```

time: 618 us -> 183 us (0.30)
  waiting for transfers between devices: 388 us -> 0 us
  Pallas kernels: 0 us -> 179 us
  local copies, waits for them, and re-layouts: 121 us -> 3.49 us
  blocking collectives: 30.4 us -> 0 us
  starting transfers between devices: 29.5 us -> 0 us
  other arithmetic: 27.4 us -> 0 us
  matrix products: 18.3 us -> 0 us
    all_to_all x4 -> x0, waiting for transfers between devices: 372 us -> none  [the longest x2 360 us: aggregate(): lax.all_to_all(outgoing, 'dom', split_axis=0, concat_axis=0, tiled=True)]
    pallas_call x0 -> x2, Pallas kernels: none -> 179 us  [the longest x1 177 us: run_all(): pl.pallas_call(whole_kernel, name='two_layers', out_shape=jax.ShapeDtypeS...]
    gather x11 -> x0, local copies, waits for them, and re-layouts: 96.7 us -> none  [the longest x1 28 us: place_blocks(): marked = jnp.take(mig_slot, holders, axis=0)]
    all_to_all x1 -> x0, blocking collectives: 30.4 us -> none  [copy_for_each(): lax.all_to_all(jnp.broadcast_to(value[None], (count, *value.shape)), axis...]
    all_to_all x4 -> x0, starting transfers between devices: 28.8 us -> none  [the longest x2 18.3 us: aggregate(): lax.all_to_all(outgoing, 'dom', split_axis=0, concat_axis=0, tiled=True)]
    dot_general x6 -> x0, matrix products: 18.3 us -> none  [the longest x2 12.1 us: aggregate(): jnp.einsum('rtij,rtjf->rif', adjacency, sources, preferred_element_type=j...]
    ppermute x2 -> x0, waiting for transfers between devices: 16 us -> none  [from_behind(): lax.ppermute(value, axis, [(i, (i + by) % count) for i in range(count)])]
    concatenate x4 -> x0, other arithmetic: 15.8 us -> none  [the longest x2 15.1 us: aggregate(): jnp.concatenate([local_blocks, arrived.reshape(-1, B, col_width)], axis=0)]
  transfers between devices with their start and end apart: 6 -> 0, of which waited for: 5 -> 0; matrix products, arithmetic and copies ran while one was open for 4% -> 0% of each run, Pallas kernels for 0% -> 0%
where the time goes in v2:
time: 183 us; the launch traced here: 182 us
  Pallas kernels  179 us (98%)
  local copies, waits for them, and re-layouts  3.49 us (2%)
    pallas_call x1, Pallas kernels, run_all(): pl.pallas_call(whole_kernel, name='two_layers', out_shape=jax.ShapeDtypeS...  177 us

profile of v2, /device:TPU:8, one launch (start us, length us, event | category | flops | bytes accessed | tf_op | source)
XLA Modules:
  0.0 182.3 jit_solution(14895940626244017835)
XLA Ops:
  0.0 0.9 copy.7
  0.9 0.1 reshape.12
  1.0 0.6 constant_dynamic-slice_fusion
  1.6 1.8 tile_tables.1.tab
  3.4 177.0 %two_layers.1 = bf16[1024,256]{1,0:T(8,128)(2,1)} custom-call(s32[40,128]{1,0:T(8,128)} %tile_tables.1.tab, s32[2,64]{1,0:T(2,128)} %bitcast.7, bf16[8,128,256]{2,1,0:T(8,128)(2,1)} %bitcast.5, bf16[128,128,128]{2,1,0:T(8,128)(2,1)} %bitcast.4, bf16[1024,1024]{1,0:T(8,128)(2,1)} %w1_ref.1, bf16[1024,1024]{1,0:T(8,128)(2,1)} %w2_ref.1), custom_call_target="tpu_custom_call" | custom-call | tf_op jit(solution)/shard_map/two_layers/pallas_call | solution.py:520
  180.4 1.9 %copy.9 = bf16[1024,256]{1,0:T(8,128)(2,1)} copy(bf16[1024,256]{1,0:T(8,128)(2,1)} %two_layers.1) | data formatting | bytes 1048576

commit v3 on v2

--- a/solution.py
+++ b/solution.py
@@ -19,9 +19,10 @@
 SLOTS = 2 * PAIRS
 QROWS = B // NY
 NP = 4
-RC = ROWS // NP
+PER = R // NP
+NE = 4
+RC = ROWS // NE
 HC = RC // 2
-PER = R // NP
 MESH = pl.DeviceIdType.MESH
 BF, F32 = jnp.bfloat16, jnp.float32
 WAYS = ((0, 1), (1, -1))
@@ -106,28 +107,29 @@
 def ring_scratch():
     n = 2 * 4 * NP
     return [pltpu.SemaphoreType.DMA((n,)), pltpu.SemaphoreType.DMA((n,))] + [
-        pltpu.SemaphoreType.DMA((NZ * NP,)),
-        pltpu.SemaphoreType.DMA((NZ * NP,)),
+        pltpu.SemaphoreType.DMA((NZ + 1,)),
+        pltpu.SemaphoreType.DMA((NZ + 1,)),
     ]
 
 
 def end_scratch():
     return [
         pltpu.VMEM((NX, ROWS, COLS), BF),
-        pltpu.VMEM((2, NP, HC, COLS), BF),
-        pltpu.VMEM((2, NP, HC, COLS), BF),
+        pltpu.VMEM((2, NE, HC, COLS), BF),
+        pltpu.VMEM((2, NE, HC, COLS), BF),
         pltpu.VMEM((2, ROWS, COLS), BF),
         pltpu.VMEM((NY, ROWS, COLS), BF),
-        pltpu.SemaphoreType.DMA((2 * NP * 3,)),
-        pltpu.SemaphoreType.DMA((2 * NP * 3,)),
-        pltpu.SemaphoreType.DMA((2 * NP * 2,)),
-        pltpu.SemaphoreType.DMA((2 * NP * 2,)),
+        pltpu.SemaphoreType.DMA((2 * NE * 3,)),
+        pltpu.SemaphoreType.DMA((2 * NE * 3,)),
+        pltpu.SemaphoreType.DMA((2 * NE * 2,)),
+        pltpu.SemaphoreType.DMA((2 * NE * 2,)),
     ]
 
 
 class Ring:
-    def __init__(self, me, blocks, own, sems):
-        self.me, self.blocks, self.own = me, blocks, own
+    def __init__(self, me, blocks, whole, sems):
+        self.me, self.blocks, self.whole = me, blocks, whole
+        self.own = lambda k: whole.at[pl.ds(k * PER, PER)]
         self.zs, self.zr, self.ss, self.sr = sems
 
     def spot(self, hops, side, k):
@@ -148,32 +150,35 @@
         i = (way * 4 + s) * NP + k
         return remote(spot, spot, self.zs.at[i], self.zr.at[i], self.me.at(dz=-1 if way == 0 else 1))
 
-    def sib_copy(self, hops, k):
-        i = (hops % NZ) * NP + k
-        return remote(
-            self.source(hops, k), self.spot(hops, 1, k), self.ss.at[i], self.sr.at[i], self.me.at(sibling=True)
-        )
-
-    def sib_arrival(self, hops, k):
-        i = (hops % NZ) * NP + k
-        spot = self.spot(hops, 1, k)
-        return remote(spot, spot, self.ss.at[i], self.sr.at[i], self.me.at(sibling=True))
+    def sib_part(self, part):
+        return (4, pl.ds(R // 2 * (part // 8), R // 2)) if part in (4, 8) else (part, pl.ds(0, R))
+
+    def sib_copy(self, part):
+        hops, rows = self.sib_part(part)
+        src = self.blocks[hops][0].at[rows] if hops else self.whole
+        dst = self.blocks[hops][1].at[rows]
+        return remote(src, dst, self.ss.at[part], self.sr.at[part], self.me.at(sibling=True))
+
+    def from_sibling(self, *parts):
+        for part in parts:
+            hops, rows = self.sib_part(part)
+            spot = self.blocks[hops][1].at[rows]
+            remote(spot, spot, self.ss.at[part], self.sr.at[part], self.me.at(sibling=True)).wait_recv()
 
     def send_own(self, k):
         for way in range(2):
             self.z_copy(way, 0, k).start()
-        self.sib_copy(0, k).start()
+        if k == NP - 1:
+            self.sib_copy(0).start()
 
     def arrive(self, way, s, k, on):
         self.z_arrival(way, s, k).wait_recv()
         if on:
             self.z_copy(way, s + 1, k).start()
-        self.sib_copy(s + 1 if way == 0 else -(s + 1), k).start()
-
-    def from_sibling(self, *hops):
-        for h in hops:
-            for k in range(NP):
-                self.sib_arrival(h, k).wait_recv()
+
+    def share(self, s):
+        for part in (s + 1, 7 - s if s < 3 else 8):
+            self.sib_copy(part).start()
 
     def finish(self):
         for way in range(2):
@@ -181,39 +186,33 @@
                 for k in range(NP):
                     if s < 3 or (k < NP // 2) == (way == 0):
                         self.z_copy(way, s, k).wait_send()
-        for h in range(NZ):
-            for k in range(NP):
-                self.sib_copy(h, k).wait_send()
+        for part in range(NZ + 1):
+            self.sib_copy(part).wait_send()
 
     def run(self, between):
+        each = NX // NP
         for s in range(4):
             if s:
-                self.from_sibling(*sorted({(s - 1) % NZ, -(s - 1) % NZ}))
-
-            def turn(k, _, ways=(0, 1), s=s):
+                self.from_sibling(*sorted({s - 1, -(s - 1) % NZ}))
+
+            def turn(k, _, ways, on, s=s):
                 for way in ways:
-                    self.arrive(way, s, k, s < 2)
+                    self.arrive(way, s, k, on[way])
                 if s:
-                    between(s - 1, k)
+                    for i in range(each):
+                        between(s - 1, k * each + i)
                 return 0
 
+            halves = ((0, NP // 2), (NP // 2, NP))
             if s < 2:
-                lax.fori_loop(0, NP, turn, 0)
-            elif s == 2:
-
-                def third(k, _, way=0):
-                    for w in range(2):
-                        self.arrive(w, 2, k, w == way)
-                    between(1, k)
-                    return 0
-
-                lax.fori_loop(0, NP // 2, third, 0)
-                lax.fori_loop(NP // 2, NP, functools.partial(third, way=1), 0)
+                lax.fori_loop(0, NP, functools.partial(turn, ways=(0, 1), on=(True, True)), 0)
             else:
-                lax.fori_loop(0, NP // 2, functools.partial(turn, ways=(0,)), 0)
-                lax.fori_loop(NP // 2, NP, functools.partial(turn, ways=(1,)), 0)
-        self.from_sibling(3, -3 % NZ)
-        self.from_sibling(4)
+                for way, (lo, hi) in enumerate(halves):
+                    on = (s == 2 and way == 0, s == 2 and way == 1)
+                    ways = (0, 1) if s == 2 else (way,)
+                    lax.fori_loop(lo, hi, functools.partial(turn, ways=ways, on=on), 0)
+            self.share(s)
+        self.from_sibling(3, 5, 4, 8)
 
 
 STEPS = (
@@ -259,8 +258,8 @@
     pl.semaphore_wait(barrier, len(partners))
 
     rings = [
-        Ring(me, blocks[0], lambda k: x_ref.at[pl.ds(k * PER, PER)], ring_sems[0]),
-        Ring(me, blocks[1], lambda k: blocks[1][0][0].at[pl.ds(k * PER, PER)], ring_sems[1]),
+        Ring(me, blocks[0], x_ref, ring_sems[0]),
+        Ring(me, blocks[1], blocks[1][0][0], ring_sems[1]),
     ]
     for k in range(NP):
         rings[0].send_own(k)
@@ -276,7 +275,7 @@
 
     def found(j, column):
         entry = tab[j, column]
-        return entry, lax.shift_right_logical(jnp.maximum(entry - 1, 0), 7)
+        return entry, jnp.bitwise_and(lax.shift_right_logical(jnp.maximum(entry - 1, 0), 7), TILES - 1)
 
     def pack(i, dx, j, _):
         for k in range(2):
@@ -360,7 +359,7 @@
         total = jnp.dot(lhs[:, :width], rhs[:width, :], preferred_element_type=F32)
         acc[rd] = total if step == 0 else acc[rd] + total
 
-    def layer_end(layer, weight, put):
+    def layer_end(layer, weight, last, put):
         part, relay_in, relay_out, sums_in, agg, xs, xr, ys, yr = ends[layer]
         halves = lambda k: (pl.ds(k * RC, HC), pl.ds(k * RC + HC, HC))
 
@@ -368,19 +367,19 @@
             rows = pl.ds(k * RC, RC)
             part[2, rows, :] = acc[2, rows, :].astype(BF)
             for way, d in WAYS:
-                i = (way * NP + k) * 3
+                i = (way * NE + k) * 3
                 go(remote(part.at[2, halves(k)[way]], relay_in.at[way, k], xs.at[i], xr.at[i], me.at(dx=d)))
 
         def x_near(k):
             for way, d in WAYS:
-                i = (way * NP + k) * 3 + 1
+                i = (way * NE + k) * 3 + 1
                 rows = halves(k)[1 - way]
                 part[d % NX, rows, :] = acc[d % NX, rows, :].astype(BF)
                 go(remote(part.at[d % NX, rows], sums_in.at[way, rows], xs.at[i], xr.at[i], me.at(dx=d)))
 
         def x_relay(k):
             for way, d in WAYS:
-                i = (way * NP + k) * 3
+                i = (way * NE + k) * 3
                 spot = relay_in.at[way, k]
                 remote(spot, spot, xs.at[i], xr.at[i], me.at(dx=-d)).wait_recv()
                 rows = halves(k)[way]
@@ -390,20 +389,20 @@
         def x_sum(k):
             for way, d in WAYS:
                 for j, rows in ((1, halves(k)[1 - way]), (2, halves(k)[way])):
-                    i = (way * NP + k) * 3 + j
+                    i = (way * NE + k) * 3 + j
                     spot = sums_in.at[way, rows]
                     remote(spot, spot, xs.at[i], xr.at[i], me.at(dx=-d)).wait_recv()
             rows = pl.ds(k * RC, RC)
             total = acc[0, rows, :] + sums_in[0, rows, :].astype(F32) + sums_in[1, rows, :].astype(F32)
             agg[me.y, rows, :] = total.astype(BF)
             for way, d in WAYS:
-                i = (way * NP + k) * 2
+                i = (way * NE + k) * 2
                 spot = agg.at[me.y, rows]
                 go(remote(spot, spot, ys.at[i], yr.at[i], me.at(dy=d)))
 
         def y_pass(k):
             for way, d in WAYS:
-                i = (way * NP + k) * 2
+                i = (way * NE + k) * 2
                 spot = agg.at[me.y_of(-d), pl.ds(k * RC, RC)]
                 remote(spot, spot, ys.at[i], yr.at[i], me.at(dy=-d)).wait_recv()
                 spot = agg.at[me.y_of(-d), halves(k)[way]]
@@ -411,7 +410,7 @@
 
         def transform(k):
             for way, d in WAYS:
-                i = (way * NP + k) * 2 + 1
+                i = (way * NE + k) * 2 + 1
                 spot = agg.at[me.y_of(2), halves(k)[way]]
                 remote(spot, spot, ys.at[i], yr.at[i], me.at(dy=-d)).wait_recv()
             total = jnp.zeros((RC, COLS), F32)
@@ -421,80 +420,94 @@
                 )
             put(k, total)
 
-        x_far(0)
-        for turn in range(NP + 3):
-            if turn + 1 < NP:
-                x_far(turn + 1)
-            if turn < NP:
-                x_near(turn)
-                x_relay(turn)
-            if 0 <= turn - 1 < NP:
+        def finish():
+            for turn in range(NE + 3):
+                if turn < NE:
+                    x_relay(turn)
+                if turn + 1 < NE:
+                    x_near(turn + 1)
+                rest(turn)
+
+        def rest(turn):
+            if 0 <= turn - 1 < NE:
                 x_sum(turn - 1)
-            if 0 <= turn - 2 < NP:
+            if 0 <= turn - 2 < NE:
                 y_pass(turn - 2)
-            if 0 <= turn - 3 < NP:
+            if 0 <= turn - 3 < NE:
                 transform(turn - 3)
+
+        last(2)
+        for k in range(NE):
+            x_far(k)
+        lax.fori_loop(0, 2, lambda i, _: last(2 * i + 1) or 0, 0)
+        x_near(0)
+        last(0)
+        finish()
 
     first = rings[0]
     both = lambda s, k: [first.arrive(way, s, k, s < 2 or (s == 2 and (k < NP // 2) == (way == 0))) for way in range(2)]
     lax.fori_loop(0, PAIRS, keep, 0)
-    both(0, 0)
-    both(0, 1)
-    tiles_from_x(0)
-    tiles_from_x(1)
-    both(0, 2)
-    both(0, 3)
-    tiles_from_x(2)
-    both(1, 0)
-    both(1, 1)
-    tiles_from_y(0)
-    both(1, 2)
-    both(1, 3)
-    tiles_from_y(1)
-    both(2, 0)
-    both(2, 1)
-    tiles_from_y(2)
-    both(2, 2)
-    both(2, 3)
+    tile_turns = [
+        lambda: (tiles_from_x(0), tiles_from_x(1)),
+        lambda: tiles_from_x(2),
+        lambda: tiles_from_y(0),
+        lambda: tiles_from_y(1),
+        lambda: tiles_from_y(2),
+    ]
+    for i in range(6):
+        for k in range(NP // 2):
+            both(i // 2, i % 2 * (NP // 2) + k)
+        if i % 2:
+            first.share(i // 2)
+        if i < len(tile_turns):
+            tile_turns[i]()
+    for i in range(3):
+        tiles_last(i)
     loads[1].wait()
+
+    def products(*steps):
+        def one(rd, _):
+            for step in steps:
+                product(0, step, rd)
+            return 0
+
+        lax.fori_loop(0, NX, one, 0)
+
+    first.from_sibling(0, 1, 7)
+    products(0, 1)
+    first.from_sibling(2, 6)
+    products(2)
     for k in range(NP):
         first.arrive(0 if k < NP // 2 else 1, 3, k, False)
-    for i in range(3):
-        tiles_last(i)
-
-    def layer_one(rd, _):
-        for step in range(4):
-            product(0, step, rd)
-        return 0
-
-    first.from_sibling(*(h for h in range(NZ) if h != 4))
-    lax.fori_loop(0, NX, layer_one, 0)
-    first.from_sibling(4)
-    lax.fori_loop(0, NX, lambda rd, _: product(0, 4, rd) or 0, 0)
+    first.share(3)
+    first.from_sibling(3, 5, 4, 8)
     loads[2].wait()
     loads[3].wait()
     second = rings[1]
 
+    per = R // NE
+
     def put_hidden(k, total):
-        hidden = jnp.maximum(total, 0.0).astype(BF).reshape(PER, B, COLS)
-        blocks[1][0][0][pl.ds(k * PER, PER)] = hidden
-        second.send_own(k)
-
-    layer_end(0, w1, put_hidden)
+        hidden = jnp.maximum(total, 0.0).astype(BF).reshape(per, B, COLS)
+        blocks[1][0][0][pl.ds(k * per, per)] = hidden
+        if (k + 1) * per % PER == 0:
+            second.send_own((k + 1) * per // PER - 1)
+
+    def last_products(layer):
+        def last(rd):
+            product(layer, 3, rd)
+            product(layer, 4, rd)
+
+        return last
+
+    layer_end(0, w1, last_products(0), put_hidden)
 
     second.run(lambda step, k: product(1, step, k))
 
-    def layer_two(rd, _):
-        product(1, 3, rd)
-        product(1, 4, rd)
-        return 0
-
-    lax.fori_loop(0, NX, layer_two, 0)
-
     def put_out(k, total):
-        done[pl.ds(k * PER, PER)] = total.astype(BF).reshape(PER, B, COLS)
-
-    layer_end(1, w2, put_out)
+        done[pl.ds(k * per, per)] = total.astype(BF).reshape(per, B, COLS)
+
+    layer_end(1, w2, last_products(1), put_out)
 
     slots = [mig[m, me.dom] for m in range(2)]
     for m in range(2):

time: 183 us -> 172 us (0.940)
  Pallas kernels: 179 us -> 167 us
    pallas_call x1, Pallas kernels: 177 us -> 165 us  [run_all(): pl.pallas_call(whole_kernel, name='two_layers', out_shape=jax.ShapeDtypeS...]
where the time goes in v3:
time: 172 us; the launch traced here: 171 us
  Pallas kernels  167 us (97%)
  local copies, waits for them, and re-layouts  3.49 us (2%)
    pallas_call x1, Pallas kernels, run_all(): pl.pallas_call(whole_kernel, name='two_layers', out_shape=jax.ShapeDtypeS...  165 us

profile of v3, /device:TPU:8, one launch (start us, length us, event | category | flops | bytes accessed | tf_op | source)
XLA Modules:
  0.0 170.7 jit_solution(7824903559668195122)
XLA Ops:
  0.0 0.9 copy.7
  0.9 0.1 reshape.12
  1.0 0.6 constant_dynamic-slice_fusion
  1.6 1.8 %tile_tables.1.tab = s32[40,128]{1,0:T(8,128)} custom-call(s32[4,128]{1,0:T(4,128)} %bitcast.6), custom_call_target="tpu_custom_call" | custom-call | tf_op jit(solution)/shard_map/tile_tables/pallas_call | solution.py:98
  3.4 165.4 %two_layers.1 = bf16[1024,256]{1,0:T(8,128)(2,1)} custom-call(s32[40,128]{1,0:T(8,128)} %tile_tables.1.tab, s32[2,64]{1,0:T(2,128)} %bitcast.7, bf16[8,128,256]{2,1,0:T(8,128)(2,1)} %bitcast.5, bf16[128,128,128]{2,1,0:T(8,128)(2,1)} %bitcast.4, bf16[1024,1024]{1,0:T(8,128)(2,1)} %w1_ref.1, bf16[1024,1024]{1,0:T(8,128)(2,1)} %w2_ref.1), custom_call_target="tpu_custom_call" | custom-call | tf_op jit(solution)/shard_map/two_layers/pallas_call | solution.py:533
  168.9 1.9 %copy.9 = bf16[1024,256]{1,0:T(8,128)(2,1)} copy(bf16[1024,256]{1,0:T(8,128)(2,1)} %two_layers.1) | data formatting | bytes 1048576

commit v4 on v3

--- a/solution.py
+++ b/solution.py
@@ -57,51 +57,40 @@
     )
 
 
-def table_kernel(src_ref, tab_ref):
+def make_tables(src_ref, tab_ref):
     x = lax.axis_index("dom") // (NZ * NC)
     t_row = lax.broadcasted_iota(jnp.int32, (1, TILES), 1)
     earlier = lax.broadcasted_iota(jnp.int32, (TILES, TILES), 0) < lax.broadcasted_iota(jnp.int32, (TILES, TILES), 1)
     lane = lax.broadcasted_iota(jnp.int32, (40, 128), 1)
     slot = lax.broadcasted_iota(jnp.int32, (40, TILES), 0)
-    total = jnp.zeros((40, 128), F32)
+    total = jnp.zeros((40, 128), jnp.int32)
 
     def ranks(i):
         s = src_ref[pl.ds(lax.rem(x + i, NX), 1), :]
         q = lax.shift_right_logical(s, 3)
         down = jnp.transpose(jnp.broadcast_to(q, (TILES, TILES)))
-        same = jnp.where(jnp.logical_and(down == q, earlier), 1.0, 0.0)
+        same = jnp.where(jnp.logical_and(down == q, earlier), 1, 0)
         return s, q, jnp.sum(same, axis=0, keepdims=True)
 
     def column(total, at, s, q, rank, col):
         here = lax.shift_right_logical(q, 4) == col
-        regular = jnp.logical_and(here, rank < 1.5)
-        more = jnp.logical_and(here, rank > 1.5)
+        regular = jnp.logical_and(here, rank < 2)
+        more = jnp.logical_and(here, rank > 1)
         first = jnp.min(jnp.where(more, t_row, TILES), axis=1, keepdims=True)
         place = jnp.where(
             regular,
-            2 * jnp.bitwise_and(q, 15) + rank.astype(jnp.int32),
+            2 * jnp.bitwise_and(q, 15) + rank,
             jnp.where(more, SLOTS - 2 + jnp.where(t_row > first, 1, 0), -1),
         )
-        entry = (1 + t_row * 128 + jnp.bitwise_and(s, 127)).astype(F32)
-        found = jnp.sum(jnp.where(slot == place, entry, 0.0), axis=1, keepdims=True)
-        return total + jnp.where(lane == at, found, 0.0)
+        entry = 1 + t_row * 128 + jnp.bitwise_and(s, 127)
+        found = jnp.sum(jnp.where(slot == place, entry, 0), axis=1, keepdims=True)
+        return total + jnp.where(lane == at, found, 0)
 
     own = ranks(0)
     for i in range(NX):
         total = column(total, i, *(own if i == 0 else ranks(i)), x)
         total = column(total, NX + i, *own, lax.rem(x + i, NX))
-    tab_ref[...] = total.astype(jnp.int32)
-
-
-def tables(sources):
-    vmem = pl.BlockSpec(memory_space=pltpu.VMEM)
-    return pl.pallas_call(
-        table_kernel,
-        name="tile_tables",
-        out_shape=jax.ShapeDtypeStruct((40, 128), jnp.int32),
-        in_specs=[vmem],
-        out_specs=vmem,
-    )(sources)
+    tab_ref[...] = total
 
 
 def ring_scratch():
@@ -224,7 +213,7 @@
 )
 
 
-def whole_kernel(tab, mig, x_ref, adj_ref, w1_ref, w2_ref, out, *refs):
+def whole_kernel(sources, mig, x_ref, adj_ref, w1_ref, w2_ref, out, *refs):
     refs = list(refs)
 
     def take(n):
@@ -236,6 +225,7 @@
     blocks = [[f[2 * h : 2 * h + 2] for h in range(NZ)] for f in flat]
     adj, tiles, send, w1, w2, acc, lhs, rhs, done, leave, came = take(11)
     loc, xs, xr, ys, yr, ms, mr = take(7)
+    made, tab = take(2)
     ring_sems = [take(4) for _ in range(2)]
     ends = [take(9) for _ in range(2)]
     me = Place()
@@ -271,6 +261,10 @@
         started.append(copy)
 
     q_rows = lambda dy: pl.ds(pl.multiple_of(me.y_of(dy) * QROWS, QROWS), QROWS)
+    make_tables(sources, made)
+    to_scalars = pltpu.make_async_copy(made, tab, loc.at[4])
+    to_scalars.start()
+    to_scalars.wait()
     loads[0].wait()
 
     def found(j, column):
@@ -525,7 +519,7 @@
         copy.wait_send()
 
 
-def run_all(tab, mig_slot, features, adjacency, weight_one, weight_two):
+def run_all(sources, mig_slot, features, adjacency, weight_one, weight_two):
     vmem = pl.BlockSpec(memory_space=pltpu.VMEM)
     smem = pl.BlockSpec(memory_space=pltpu.SMEM)
     hbm = pl.BlockSpec(memory_space=pl.ANY)
@@ -534,7 +528,7 @@
         whole_kernel,
         name="two_layers",
         out_shape=jax.ShapeDtypeStruct((ROWS, COLS), BF),
-        in_specs=[smem, smem, hbm, hbm, hbm, hbm],
+        in_specs=[vmem, smem, hbm, hbm, hbm, hbm],
         out_specs=vmem,
         scratch_shapes=[pltpu.VMEM((R, B, COLS), BF)] * (4 * NZ)
         + [
@@ -549,20 +543,22 @@
             pltpu.VMEM((R + 2, B, COLS), BF),
             pltpu.VMEM((2, B, COLS), BF),
             pltpu.VMEM((2, B, COLS), BF),
-            dma((4,)),
+            dma((5,)),
             dma((3,)),
             dma((3,)),
             dma((12,)),
             dma((12,)),
             dma,
             dma,
+            pltpu.VMEM((40, 128), jnp.int32),
+            pltpu.SMEM((40, 128), jnp.int32),
         ]
         + ring_scratch() * 2
         + end_scratch() * 2,
         compiler_params=pltpu.CompilerParams(
             collective_id=0, has_side_effects=True, vmem_limit_bytes=60 * 1024 * 1024
         ),
-    )(tab, mig_slot.T, features, adjacency, weight_one, weight_two)
+    )(sources, mig_slot.T, features, adjacency, weight_one, weight_two)
 
 
 def on_device(features, adjacency, tile_src, mig_slot, weight_one, weight_two):
@@ -570,9 +566,8 @@
     z, c = lax.rem(lax.div(dom, NC), NZ), lax.rem(dom, NC)
     grid = tile_src.reshape(NX, NZ, NC, TILES)
     sources = lax.dynamic_slice(grid, (0, z, c, 0), (NX, 1, 1, TILES)).reshape(NX, TILES)
-    tab = tables(sources)
     return run_all(
-        tab, mig_slot, features.reshape(R, B, COLS), adjacency.reshape(TILES, B, B), weight_one, weight_two
+        sources, mig_slot, features.reshape(R, B, COLS), adjacency.reshape(TILES, B, B), weight_one, weight_two
     )
 
 

time: 172 us -> 170 us (0.988)
  Pallas kernels: 167 us -> 165 us
    pallas_call x1 -> x0, Pallas kernels: 1.81 us -> none  [tables(): pl.pallas_call(table_kernel, name='tile_tables', out_shape=jax.ShapeDtype...]
where the time goes in v4:
time: 170 us; the launch traced here: 169 us
  Pallas kernels  165 us (97%)
  local copies, waits for them, and re-layouts  3.48 us (2%)
    pallas_call x1, Pallas kernels, run_all(): pl.pallas_call(whole_kernel, name='two_layers', out_shape=jax.ShapeDtypeS...  165 us

profile of v4, /device:TPU:8, one launch (start us, length us, event | category | flops | bytes accessed | tf_op | source)
XLA Modules:
  0.0 168.8 jit_solution(9708079571016363004)
XLA Ops:
  0.0 0.9 copy.7
  0.9 0.1 reshape.12
  1.0 0.6 constant_dynamic-slice_fusion
  1.6 165.3 %two_layers.1 = bf16[1024,256]{1,0:T(8,128)(2,1)} custom-call(s32[4,128]{1,0:T(4,128)} %bitcast.6, s32[2,64]{1,0:T(2,128)} %bitcast.7, bf16[8,128,256]{2,1,0:T(8,128)(2,1)} %bitcast.5, bf16[128,128,128]{2,1,0:T(8,128)(2,1)} %bitcast.4, bf16[1024,1024]{1,0:T(8,128)(2,1)} %w1_ref.1, bf16[1024,1024]{1,0:T(8,128)(2,1)} %w2_ref.1), custom_call_target="tpu_custom_call" | custom-call | tf_op jit(solution)/shard_map/two_layers/pallas_call | solution.py:527
  166.9 1.9 %copy.9 = bf16[1024,256]{1,0:T(8,128)(2,1)} copy(bf16[1024,256]{1,0:T(8,128)(2,1)} %two_layers.1) | data formatting | bytes 1048576

commit v5 on v4

--- a/solution.py
+++ b/solution.py
@@ -201,7 +201,7 @@
                     ways = (0, 1) if s == 2 else (way,)
                     lax.fori_loop(lo, hi, functools.partial(turn, ways=ways, on=on), 0)
             self.share(s)
-        self.from_sibling(3, 5, 4, 8)
+        self.from_sibling(3, 5)
 
 
 STEPS = (
@@ -474,7 +474,7 @@
     for k in range(NP):
         first.arrive(0 if k < NP // 2 else 1, 3, k, False)
     first.share(3)
-    first.from_sibling(3, 5, 4, 8)
+    first.from_sibling(3, 5)
     loads[2].wait()
     loads[3].wait()
     second = rings[1]
@@ -490,6 +490,8 @@
     def last_products(layer):
         def last(rd):
             product(layer, 3, rd)
+            if isinstance(rd, int) and rd == 2:
+                rings[layer].from_sibling(4, 8)
             product(layer, 4, rd)
 
         return last

time: 170 us -> 172 us (1.012)
  Pallas kernels: 165 us -> 167 us
    pallas_call x1, Pallas kernels: 165 us -> 167 us  [run_all(): pl.pallas_call(whole_kernel, name='two_layers', out_shape=jax.ShapeDtypeS...]
where the time goes in v5:
time: 172 us; the launch traced here: 171 us
  Pallas kernels  167 us (97%)
  local copies, waits for them, and re-layouts  3.48 us (2%)
    pallas_call x1, Pallas kernels, run_all(): pl.pallas_call(whole_kernel, name='two_layers', out_shape=jax.ShapeDtypeS...  167 us

profile of v5, /device:TPU:8, one launch (start us, length us, event | category | flops | bytes accessed | tf_op | source)
XLA Modules:
  0.0 171.0 jit_solution(13673919771825480970)
XLA Ops:
  0.0 0.9 copy.7
  0.9 0.1 reshape.12
  1.0 0.6 constant_dynamic-slice_fusion
  1.6 167.5 %two_layers.1 = bf16[1024,256]{1,0:T(8,128)(2,1)} custom-call(s32[4,128]{1,0:T(4,128)} %bitcast.6, s32[2,64]{1,0:T(2,128)} %bitcast.7, bf16[8,128,256]{2,1,0:T(8,128)(2,1)} %bitcast.5, bf16[128,128,128]{2,1,0:T(8,128)(2,1)} %bitcast.4, bf16[1024,1024]{1,0:T(8,128)(2,1)} %w1_ref.1, bf16[1024,1024]{1,0:T(8,128)(2,1)} %w2_ref.1), custom_call_target="tpu_custom_call" | custom-call | tf_op jit(solution)/shard_map/two_layers/pallas_call | solution.py:529
  169.1 1.9 %copy.9 = bf16[1024,256]{1,0:T(8,128)(2,1)} copy(bf16[1024,256]{1,0:T(8,128)(2,1)} %two_layers.1) | data formatting | bytes 1048576
